TPU v7x, 128 devices: a whole 4x4x4 slice. The times are simulated.
128 devices in a mesh: rec: 4 (over x_lo, core), ch: 32 (over y, z, x_hi).
Axes of the slice: x: 4 (x_hi: 2, x_lo: 2; x = x_hi * 2 + x_lo), y: 4, z: 4, core: 2. Of those that a mesh axis runs over, the one named last changes fastest.
Arguments:
- samples: bfloat16 [4, 4, 1280, 6144], P('rec', None, 'ch')
- source_ids: int32 [8], replicated, may hold values from 0 to 5119
Outputs:
- correlations: float32 [8, 5120, 6144], P(None, ('rec', 'ch'))
All inputs are finite; a program needn't handle non-finite values.
Results may differ from a plain program's by a relative error of at most 0.0003.
Values may be sent and summed in bfloat16 or wider, within the bound.
A program may use at most 128 MiB of HBM per device.

v0:
```python
import math

import jax
import jax.numpy as jnp
from jax import lax
from jax.sharding import PartitionSpec as P

NFFT = 6144
BAND = 64
NSRC = 8


epsilon = 1e-06
precise = lax.Precision.HIGHEST


def rotations(rows, cols, period):
    row_index = jnp.arange(rows, dtype=jnp.int32)[:, None]
    col_index = jnp.arange(cols, dtype=jnp.int32)[None, :]
    angles = (row_index * col_index % period).astype(jnp.float32) * (2.0 * math.pi / period)
    return (jnp.cos(angles), jnp.sin(angles))


def transform(real_part, imag_part, total, keep_imag):
    inner_size = 128
    outer_size = total // inner_size
    leading = real_part.shape[:-1]
    cos_inner, sin_inner = rotations(inner_size, inner_size, inner_size)
    cos_twist, sin_twist = rotations(outer_size, inner_size, total)
    cos_outer, sin_outer = rotations(outer_size, outer_size, outer_size)
    shaped = real_part.reshape(leading + (inner_size, outer_size))
    segment_real = jnp.einsum("...qp,qk->...pk", shaped, cos_inner, precision=precise)
    segment_imag = -jnp.einsum("...qp,qk->...pk", shaped, sin_inner, precision=precise)
    if imag_part is not None:
        shaped_imag = imag_part.reshape(leading + (inner_size, outer_size))
        segment_real = segment_real + jnp.einsum(
            "...qp,qk->...pk", shaped_imag, sin_inner, precision=precise
        )
        segment_imag = segment_imag + jnp.einsum(
            "...qp,qk->...pk", shaped_imag, cos_inner, precision=precise
        )
    twist_real = segment_real * cos_twist + segment_imag * sin_twist
    twist_imag = segment_imag * cos_twist - segment_real * sin_twist
    out_real = jnp.einsum("...pk,pj->...jk", twist_real, cos_outer, precision=precise)
    out_real = out_real + jnp.einsum("...pk,pj->...jk", twist_imag, sin_outer, precision=precise)
    out_real = out_real.reshape(leading + (total,))
    if not keep_imag:
        return (out_real, None)
    out_imag = jnp.einsum("...pk,pj->...jk", twist_imag, cos_outer, precision=precise)
    out_imag = out_imag - jnp.einsum("...pk,pj->...jk", twist_real, sin_outer, precision=precise)
    return (out_real, out_imag.reshape(leading + (total,)))


def whiten(real_part, imag_part):
    energy = real_part * real_part + imag_part * imag_part
    leading = energy.shape[:-1]
    band_mean = (
        jnp.mean(energy.reshape(leading + (NFFT // BAND, BAND)), axis=-1, keepdims=True) + epsilon
    )
    factor = jnp.broadcast_to(lax.rsqrt(band_mean), leading + (NFFT // BAND, BAND)).reshape(
        leading + (NFFT,)
    )
    return (real_part * factor, imag_part * factor)


def spectra(received):
    fiber_rows = received[:, 0]
    spec_real, spec_imag = transform(fiber_rows.astype(jnp.float32), None, NFFT, True)
    white_real, white_imag = whiten(spec_real, spec_imag)
    return (white_real, white_imag, fiber_rows)


def shards(samples, source_ids):
    channels = samples.shape[2]
    white_real, white_imag, fiber_rows = spectra(
        lax.all_to_all(samples, "rec", split_axis=1, concat_axis=0, tiled=True)
    )
    windows = white_real.shape[0]
    first_channel = lax.axis_index(("rec", "ch")) * channels
    local_ids = first_channel + jnp.arange(channels, dtype=jnp.int32)
    chooser = (source_ids[:, None] == local_ids[None, :]).astype(jnp.float32)
    source_real = jnp.einsum("sc,wcf->swf", chooser, white_real, precision=precise)
    source_imag = jnp.einsum("sc,wcf->swf", chooser, white_imag, precision=precise)
    source_real, source_imag = lax.psum((source_real, source_imag), ("rec", "ch"))

    def accumulate(window, totals):
        cross_real, cross_imag = totals
        left_real = lax.dynamic_index_in_dim(source_real, window, 1, keepdims=False)[:, None, :]
        left_imag = lax.dynamic_index_in_dim(source_imag, window, 1, keepdims=False)[:, None, :]
        right_real = lax.dynamic_index_in_dim(white_real, window, 0, keepdims=False)[None]
        right_imag = lax.dynamic_index_in_dim(white_imag, window, 0, keepdims=False)[None]
        cross_real = cross_real + left_real * right_real + left_imag * right_imag
        cross_imag = cross_imag + left_imag * right_real - left_real * right_imag
        return (cross_real, cross_imag)

    empty = jnp.zeros((NSRC, channels, NFFT), jnp.float32)
    cross_real, cross_imag = lax.fori_loop(0, windows, accumulate, (empty, empty))
    lagged, unused = transform(cross_real, -cross_imag, NFFT, False)
    lagged = lagged * (1.0 / math.sqrt(windows * NFFT))
    midpoint = NFFT // 2
    return jnp.concatenate((lagged[..., midpoint:], lagged[..., :midpoint]), axis=-1)


def solution(mesh):
    return jax.shard_map(
        shards,
        mesh=mesh,
        in_specs=(P("rec", None, "ch", None), P()),
        out_specs=P(None, ("rec", "ch"), None),
        check_vma=False,
    )
```

profile of v0, /device:TPU:1, one launch (start us, length us, event | category | flops | bytes accessed | tf_op | source)
XLA Modules:
  0.0 569.2 jit_solution(9517593881424919913)
XLA Ops:
  6.5 5.0 all-to-all-start
  11.6 23.3 %all-to-all-done = bf16[1,4,40,6144]{3,2,0,1:T(8,128)(2,1)S(1)} async-done(((bf16[1,4,40,6144]{3,2,0,1:T(8,128)(2,1)}), bf16[1,4,40,6144]{3,2,0,1:T(8,128)(2,1)S(1)}, u32[]{:S(2)}, u32[]{:S(2)}) %all-to-all-start) | async-done | bytes 1966112 | tf_op jit(solution)/shard_map/all_to_all | solution.py:76
  34.9 6.4 %reshape.76 = bf16[4,40,128,48]{3,2,1,0:T(8,128)(2,1)} reshape(bf16[1,4,40,6144]{3,2,0,1:T(8,128)(2,1)S(1)} %all-to-all-done) | data formatting | bytes 3932160 | tf_op jit(solution)/shard_map/reshape | solution.py:31
  41.3 7.0 %fusion.32 = f32[128,4,40,48]{0,3,2,1:T(8,128)S(1)} fusion(bf16[4,40,128,48]{3,2,1,0:T(8,128)(2,1)} %reshape.76), kind=kOutput, calls=%fused_computation.46 | convolution fusion | flops 1510178816 | bytes 5898240 | tf_op jit(solution)/shard_map/...qp,qk->...pk/dot_general | solution.py:32
  48.4 4.4 fusion.38
  52.8 3.9 fusion.24
  56.7 5.8 %fusion.20 = f32[48,4,40,128]{3,0,2,1:T(8,128)} fusion(f32[128,4,40,48]{0,3,2,1:T(8,128)S(1)} %fusion.32, f32[128,4,40,48]{0,3,2,1:T(8,128)S(1)} %fusion.38, f32[48,128]{1,0:T(8,128)S(1)} %get-tuple-element.184, f32[48,128]{1,0:T(8,128)S(1)} %get-tuple-element.185), kind=kOutput, calls=%fused_computation.34 | convolution fusion | flops 570183936 | bytes 11845632 | tf_op jit(solution)/shard_map/...pk,pj->...jk/dot_general | solution.py:49
  62.5 5.8 %add_bitcast_fusion = f32[4,40,48,128]{3,2,1,0:T(8,128)} fusion(f32[48,4,40,128]{3,0,2,1:T(8,128)S(1)} %fusion.24, f32[128,4,40,48]{0,3,2,1:T(8,128)S(1)} %fusion.32, f32[128,4,40,48]{0,3,2,1:T(8,128)S(1)} %fusion.38, f32[48,128]{1,0:T(8,128)S(1)} %get-tuple-element.184, f32[48,128]{1,0:T(8,128)S(1)} %get-tuple-element.185), kind=kOutput, calls=%fused_computation.31 | convolution fusion | flops 571166976 | bytes 15777792 | tf_op jit(solution)/shard_map/...pk,pj->...jk/dot_general | solution.py:45
  68.3 5.0 reshape.77
  73.2 12.7 %multiply_add_fusion = (f32[4,40,48,128]{3,2,1,0:T(8,128)}, f32[4,40,48,128]{3,2,1,0:T(8,128)}) fusion(f32[4,40,48,128]{3,2,1,0:T(8,128)} %add_bitcast_fusion, f32[48,4,40,128]{3,0,2,1:T(8,128)} %fusion.20, f32[128,4,40,48]{0,3,2,1:T(8,128)} %copy-done.1, f32[128,4,40,48]{0,3,2,1:T(8,128)} %copy-done.2, f32[48,128]{1,0:T(8,128)S(1)} %get-tuple-element.184, ...), kind=kOutput, calls=%fused_computation.29 | convolution fusion | flops 574116096 | bytes 23642112 | tf_op jit(solution)/shard_map/...pk,pj->...jk/dot_general | solution.py:50
  86.0 6.6 %add.179 = f32[4,40,96,64]{3,2,1,0:T(8,128)} reshape(f32[4,40,48,128]{3,2,1,0:T(8,128)} %get-tuple-element.182) | data formatting | bytes 7864320 | tf_op jit(solution)/shard_map/add | solution.py:55
  92.6 6.0 %reduce_sum.9 = f32[4,40,96]{2,1,0:T(8,128)S(1)} reduce(f32[4,40,96,64]{3,2,1,0:T(8,128)} %add.179, f32[]{:T(128)} %constant.94.clone.1), dimensions={3}, to_apply=%region_0.1 | reduce | flops 967680 | bytes 3993604 | tf_op jit(solution)/shard_map/reduce_sum | solution.py:58
  98.7 4.9 broadcast_in_dim.5
  103.5 7.8 %reshape.78 = f32[4,40,6144]{2,1,0:T(8,128)} reshape(f32[4,40,96,64]{3,2,1,0:T(8,128)} %broadcast_in_dim.5) | data formatting | bytes 7864320 | tf_op jit(solution)/shard_map/reshape | solution.py:60
  111.3 5.3 reshape.79
  116.6 5.2 fusion.148
  128.3 151.8 %all-reduce.3.cloned.1.call-done = (f32[8,4,6144]{2,0,1:T(8,128)}, f32[8,4,6144]{2,0,1:T(8,128)}) async-done(((f32[8,4,6144]{2,0,1:T(8,128)}, f32[8,4,6144]{2,0,1:T(8,128)}), (f32[8,4,6144]{2,0,1:T(8,128)}, f32[8,4,6144]{2,0,1:T(8,128)})) %all-reduce.3.cloned.1.call-update) | async-done | bytes 1572880 | tf_op jit(solution)/shard_map/psum | solution.py:84
  280.1 50.3 %while.16 = (s32[]{:T(128)}, f32[8,40,6144]{2,1,0:T(8,128)}, f32[8,40,6144]{2,1,0:T(8,128)}, f32[8,4,6144]{2,0,1:T(8,128)}, f32[4,40,6144]{2,1,0:T(8,128)}, /*in...) while((s32[]{:T(128)}, f32[8,40,6144]{2,1,0:T(8,128)}, ...), condition=%wide.region_4.5_spmd.clone, body=%wide.region_3.4_spmd.clone.sunk | while | flops 19660804 | bytes 38535276 | solution.py:97
  282.8 7.4 %fusion.158 = (f32[8,40,6144]{2,1,0:T(8,128)}, f32[8,40,6144]{2,1,0:T(8,128)}) fusion(f32[8,40,6144]{2,1,0:T(8,128)} %get-tuple-element.253, f32[40,6144]{1,0:T(8,128)S(1)} %get-tuple-element.236, f32[8,6144]{1,0:T(8,128)S(1)} %get-tuple-element.237, f32[40,6144]{1,0:T(8,128)S(1)} %get-tuple-element.238, f32[8,6144]{1,0:T(8,128)S(1)} %get-tuple-element.239, ...), kind=kLoop, calls=%fused_computation.1.clone.1 | loop fusion | flops 19660800 | bytes 33816576 | tf_op jit(solution)/shard_map/while/body/eval_jaxpr/sub | solution.py:93
  292.9 10.7 %fusion.158 = (f32[8,40,6144]{2,1,0:T(8,128)}, f32[8,40,6144]{2,1,0:T(8,128)}) fusion(f32[8,40,6144]{2,1,0:T(8,128)} %get-tuple-element.253, f32[40,6144]{1,0:T(8,128)S(1)} %get-tuple-element.236, f32[8,6144]{1,0:T(8,128)S(1)} %get-tuple-element.237, f32[40,6144]{1,0:T(8,128)S(1)} %get-tuple-element.238, f32[8,6144]{1,0:T(8,128)S(1)} %get-tuple-element.239, ...), kind=kLoop, calls=%fused_computation.1.clone.1 | loop fusion | flops 19660800 | bytes 33816576 | tf_op jit(solution)/shard_map/while/body/eval_jaxpr/sub | solution.py:93
  306.3 10.7 %fusion.158 = (f32[8,40,6144]{2,1,0:T(8,128)}, f32[8,40,6144]{2,1,0:T(8,128)}) fusion(f32[8,40,6144]{2,1,0:T(8,128)} %get-tuple-element.253, f32[40,6144]{1,0:T(8,128)S(1)} %get-tuple-element.236, f32[8,6144]{1,0:T(8,128)S(1)} %get-tuple-element.237, f32[40,6144]{1,0:T(8,128)S(1)} %get-tuple-element.238, f32[8,6144]{1,0:T(8,128)S(1)} %get-tuple-element.239, ...), kind=kLoop, calls=%fused_computation.1.clone.1 | loop fusion | flops 19660800 | bytes 33816576 | tf_op jit(solution)/shard_map/while/body/eval_jaxpr/sub | solution.py:93
  319.8 10.7 %fusion.158 = (f32[8,40,6144]{2,1,0:T(8,128)}, f32[8,40,6144]{2,1,0:T(8,128)}) fusion(f32[8,40,6144]{2,1,0:T(8,128)} %get-tuple-element.253, f32[40,6144]{1,0:T(8,128)S(1)} %get-tuple-element.236, f32[8,6144]{1,0:T(8,128)S(1)} %get-tuple-element.237, f32[40,6144]{1,0:T(8,128)S(1)} %get-tuple-element.238, f32[8,6144]{1,0:T(8,128)S(1)} %get-tuple-element.239, ...), kind=kLoop, calls=%fused_computation.1.clone.1 | loop fusion | flops 19660800 | bytes 33816576 | tf_op jit(solution)/shard_map/while/body/eval_jaxpr/sub | solution.py:93
  330.4 16.4 %reshape.80 = f32[8,40,128,48]{3,2,1,0:T(8,128)} reshape(f32[8,40,6144]{2,1,0:T(8,128)} %get-tuple-element.130) | data formatting | bytes 15728640 | tf_op jit(solution)/shard_map/reshape | solution.py:31
  346.9 37.5 %fusion.34 = f32[8,40,48,128]{3,2,1,0:T(8,128)} fusion(f32[8,40,128,48]{3,2,1,0:T(8,128)} %reshape.80), kind=kOutput, calls=%fused_computation.48 | convolution fusion | flops 3020128256 | bytes 15728640 | tf_op jit(solution)/shard_map/...qp,qk->...pk/dot_general | solution.py:33
  384.3 37.5 %fusion.30 = f32[8,40,48,128]{3,2,1,0:T(8,128)} fusion(f32[8,40,128,48]{3,2,1,0:T(8,128)} %reshape.80), kind=kOutput, calls=%fused_computation.44 | convolution fusion | flops 3020128256 | bytes 15728640 | tf_op jit(solution)/shard_map/...qp,qk->...pk/dot_general | solution.py:32
  425.5 16.4 %reshape.81 = f32[8,40,128,48]{3,2,1,0:T(8,128)} reshape(f32[8,40,6144]{2,1,0:T(8,128)} %neg.14) | data formatting | bytes 15728640 | tf_op jit(solution)/shard_map/reshape | solution.py:35
  442.0 38.8 %fusion.36 = f32[8,40,48,128]{3,2,1,0:T(8,128)} fusion(f32[8,40,128,48]{3,2,1,0:T(8,128)} %reshape.81), kind=kOutput, calls=%fused_computation.50 | convolution fusion | flops 3020128256 | bytes 15728640 | tf_op jit(solution)/shard_map/...qp,qk->...pk/dot_general | solution.py:36
  480.7 37.9 %negate_add_fusion = f32[8,40,48,128]{3,2,1,0:T(8,128)} fusion(f32[8,40,48,128]{3,2,1,0:T(8,128)} %fusion.34, f32[8,40,128,48]{3,2,1,0:T(8,128)S(1)} %copy-done), kind=kOutput, calls=%fused_computation.17 | convolution fusion | flops 3024060416 | bytes 23592960 | tf_op jit(solution)/shard_map/...qp,qk->...pk/dot_general | solution.py:39
  518.6 12.8 %fusion.2 = f32[48,8,40,128]{3,0,2,1:T(8,128)} fusion(f32[8,40,48,128]{3,2,1,0:T(8,128)} %negate_add_fusion, f32[48,128]{1,0:T(8,128)S(1)} %get-tuple-element.184, f32[48,128]{1,0:T(8,128)S(1)} %get-tuple-element.185, f32[8,40,48,128]{3,2,1,0:T(8,128)S(1)} %bitcast.113, f32[8,40,48,128]{3,2,1,0:T(8,128)} %fusion.36), kind=kOutput, calls=%fused_computation.10 | convolution fusion | flops 1140347136 | bytes 31506432 | tf_op jit(solution)/shard_map/...pk,pj->...jk/dot_general | solution.py:45
  531.5 14.3 %multiply_bitcast_fusion = f32[8,40,48,128]{3,2,1,0:T(8,128)} fusion(f32[48,8,40,128]{3,0,2,1:T(8,128)} %fusion.2, f32[8,40,48,128]{3,2,1,0:T(8,128)} %negate_add_fusion, f32[48,128]{1,0:T(8,128)S(1)} %get-tuple-element.184, f32[48,128]{1,0:T(8,128)S(1)} %get-tuple-element.185, f32[8,40,48,128]{3,2,1,0:T(8,128)S(1)} %bitcast.113, f32[8,40,48,128]{3,2,1,0:T(8,128)} %fusion.36), kind=kOutput, calls=%fused_computation.9 | convolution fusion | flops 1144279296 | bytes 39370752 | tf_op jit(solution)/shard_map/...pk,pj->...jk/dot_general | solution.py:44
  545.7 9.0 %mul.461 = f32[8,40,6144]{2,1,0:T(8,128)} reshape(f32[8,40,48,128]{3,2,1,0:T(8,128)} %multiply_bitcast_fusion) | data formatting | bytes 15728640 | tf_op jit(solution)/shard_map/mul | solution.py:99
  554.7 7.5 %fusion.147 = (f32[8,40,6144]{2,1,0:T(8,128)}, f32[8,40,6144]{2,1,0:T(8,128)}) fusion(f32[8,40,6144]{2,1,0:T(8,128)} %mul.461, f32[8,40,6144]{2,1,0:T(8,128)} %custom-call.2), kind=kLoop, output_to_operand_aliasing={{0}: (1, {}), {1}: (1, {})}, calls=%fused_computation.148 | loop fusion | bytes 15728640 | tf_op jit(solution)/shard_map/slice | solution.py:101
  (43 shorter events, 21.1 us)
Async XLA Ops:
  6.5 28.4 %all-to-all-start = ((bf16[1,4,40,6144]{3,2,0,1:T(8,128)(2,1)}), bf16[1,4,40,6144]{3,2,0,1:T(8,128)(2,1)S(1)}, u32[]{:S(2)}, u32[]{:S(2)}) async-start(bf16[1,4,40,6144]{3,2,0,1:T(8,128)(2,1)} %bitcast.114), calls=%async_computation | async-start | bytes 3932160 | tf_op jit(solution)/shard_map/all_to_all | solution.py:76
  11.5 268.6 %all-reduce.3.cloned.1.call-start = ((), (), s32[]{:S(2)}) async-start(), calls=%async_computation.1 | async-start | bytes 3145728 | tf_op jit(solution)/shard_map/psum | solution.py:84
  41.3 7.0 %copy-start.3 = (bf16[4,40,128,48]{3,2,1,0:T(8,128)(2,1)S(1)}, bf16[4,40,128,48]{3,2,1,0:T(8,128)(2,1)}, u32[]{:S(2)}) copy-start(bf16[4,40,128,48]{3,2,1,0:T(8,128)(2,1)} %reshape.76) | copy-start | bytes 5898244
  48.4 14.1 %copy-start.1 = (f32[128,4,40,48]{0,3,2,1:T(8,128)}, f32[128,4,40,48]{0,3,2,1:T(8,128)S(1)}, u32[]{:S(2)}) copy-start(f32[128,4,40,48]{0,3,2,1:T(8,128)S(1)} %fusion.32) | copy-start | bytes 11796484
  52.8 9.7 %copy-start.2 = (f32[128,4,40,48]{0,3,2,1:T(8,128)}, f32[128,4,40,48]{0,3,2,1:T(8,128)S(1)}, u32[]{:S(2)}) copy-start(f32[128,4,40,48]{0,3,2,1:T(8,128)S(1)} %fusion.38) | copy-start | bytes 11796484
  116.6 7.1 %copy-start.6 = (s32[8]{0:T(128)S(1)}, s32[8]{0:T(128)}, u32[]{:S(2)}) copy-start(s32[8]{0:T(128)} %param.5) | copy-start | bytes 100
  121.8 1.9 copy-start.4
  121.8 4.2 copy-start.5
  346.9 75.0 %slice-start = ((s8[7864320]{0:T(1024)(128)(4,1)}), s8[4194304]{0:T(1024)(128)(4,1)S(1)}, s32[]{:S(2)}) async-start(s8[7864320]{0:T(1024)(128)(4,1)} %bitcast.110), calls=%async_computation.2 | async-start | bytes 8388608
  384.3 37.5 %slice-start.1 = ((s8[7864320]{0:T(1024)(128)(4,1)}), s8[3670016]{0:T(1024)(128)(4,1)S(1)}, s32[]{:S(2)}) async-start(s8[7864320]{0:T(1024)(128)(4,1)} %bitcast.110), calls=%async_computation.3 | async-start | bytes 7340032
  442.0 38.8 %copy-start = (f32[8,40,128,48]{3,2,1,0:T(8,128)S(1)}, f32[8,40,128,48]{3,2,1,0:T(8,128)}, u32[]{:S(2)}) copy-start(f32[8,40,128,48]{3,2,1,0:T(8,128)} %reshape.81) | copy-start | bytes 23592964
  442.0 76.7 %slice-start.2 = ((s8[7864320]{0:T(1024)(128)(4,1)}), s8[4194304]{0:T(1024)(128)(4,1)S(1)}, s32[]{:S(2)}) async-start(s8[7864320]{0:T(1024)(128)(4,1)} %bitcast.112), calls=%async_computation.4 | async-start | bytes 8388608
  480.7 37.9 %slice-start.3 = ((s8[7864320]{0:T(1024)(128)(4,1)}), s8[3670016]{0:T(1024)(128)(4,1)S(1)}, s32[]{:S(2)}) async-start(s8[7864320]{0:T(1024)(128)(4,1)} %bitcast.112), calls=%async_computation.5 | async-start | bytes 7340032
Sparse Core Ops, SparseCore 0:
  128.4 151.6 all-reduce.2
where the time goes:
time: 574 us; the launch traced here: 569 us
  matrix products  223 us (39%)
  waiting for transfers between devices  175 us (30%)
  local copies, waits for them, and re-layouts  97.9 us (17%)
  other arithmetic  54.5 us (9%)
  between operations  13.8 us (2%)
    psum x1, waiting for transfers between devices, shards(): lax.psum((source_real, source_imag), ('rec', 'ch'))  152 us
    dot_general x2, matrix products, transform(): jnp.einsum('...qp,qk->...pk', shaped, cos_inner, precision=precise)  44.5 us
    dot_general x2, matrix products, transform(): jnp.einsum('...qp,qk->...pk', shaped, sin_inner, precision=precise)  41.9 us
    sub x4, other arithmetic, accumulate(): cross_imag = cross_imag + left_imag * right_real - left_real * right_imag  39.5 us
    dot_general x1, matrix products, transform(): jnp.einsum('...qp,qk->...pk', shaped_imag, sin_inner, precision=precise)  38.8 us
    dot_general x1, matrix products, transform(): jnp.einsum('...qp,qk->...pk', shaped_imag, cos_inner, precision=precise)  37.9 us
    all_to_all x1, waiting for transfers between devices, shards(): lax.all_to_all(samples, 'rec', split_axis=1, concat_axis=0, tiled=True)  23.3 us
    reshape x2, local copies, waits for them, and re-layouts, transform(): shaped = real_part.reshape(leading + (inner_size, outer_size))  22.8 us
  transfers between devices with their start and end apart: 2, of which 2 were waited for; matrix products, arithmetic and copies ran while one was open for 0% of the time, Pallas kernels for 0%

commit v1 on v0

v1 whole, which is shorter than its diff:
```python
import math
import numpy as np
import jax
import jax.numpy as jnp
from jax import lax
from jax.experimental import pallas as pl
from jax.experimental.pallas import tpu as pltpu
from jax.sharding import PartitionSpec as P

NFFT = 6144
SLOW = 48
FAST = 128
HALF = 25
NSRC = 8
NWIN = 4
EPS = 1e-06
ROWS = HALF * 16


def split_bf16(a):
    hi = a.astype(jnp.bfloat16)
    lo = (np.asarray(a, np.float32) - hi.astype(np.float32)).astype(jnp.bfloat16)
    return hi, lo


def tables():
    n = np.arange(FAST)
    ang = 2.0 * np.pi * ((n[:, None] * n[None, :]) % FAST) / FAST
    c, s = np.cos(ang), np.sin(ang)
    forward = np.block([[c, -s], [s, c]]).astype(np.float32)
    inverse = np.block([[c, s], [-s, c]]).astype(np.float32)
    fhi, flo = split_bf16(forward)
    ihi, ilo = split_bf16(inverse)
    fw = np.concatenate([fhi, flo], axis=0)
    iv = np.concatenate([ihi, ilo], axis=0)
    k1 = np.arange(HALF)[:, None]
    turn = 2.0 * np.pi * (k1 * n[None, :]) / NFFT
    scale = ((-1.0) ** k1) / math.sqrt(NWIN * NFFT) * np.where((k1 == 0) | (k1 == SLOW // 2), 1.0, 0.5)
    tw = np.stack([np.cos(turn), np.sin(turn), np.cos(turn) * scale, np.sin(turn) * scale], axis=1)
    tw = np.broadcast_to(tw[:, :, None, :], (HALF, 4, 8, FAST)).astype(np.float32)
    return fw, iv, np.ascontiguousarray(tw)


class V:
    def __init__(self, x, neg=False):
        self.x, self.neg = x, neg

    def __neg__(self):
        return V(self.x, not self.neg)

    def __add__(self, o):
        if self.neg == o.neg:
            return V(self.x + o.x, self.neg)
        return V(o.x - self.x) if self.neg else V(self.x - o.x)

    def __sub__(self, o):
        return self + (-o)

    def scale(self, f):
        if abs(f - 1.0) < 1e-12:
            return self
        return V(self.x * np.float32(abs(f)), self.neg != (f < 0))

    def get(self):
        return -self.x if self.neg else self.x


def turned(z, quarter, size):
    re, im = z
    step = (quarter * (16 // size)) % 16
    if step == 0:
        return z
    if step == 4:
        return im, -re
    if step == 12:
        return -im, re
    if step == 8:
        return -re, -im
    root = math.sqrt(0.5)
    if step == 2:
        return (re + im).scale(root), (im - re).scale(root)
    if step == 14:
        return (re - im).scale(root), (im + re).scale(root)
    c, s = math.cos(2 * math.pi * step / 16), math.sin(2 * math.pi * step / 16)
    return re.scale(c) + im.scale(s), im.scale(c) - re.scale(s)


def rfft(xs):
    n = len(xs)
    if n == 2:
        return [(xs[0] + xs[1], None), (xs[0] - xs[1], None)]
    even, odd = rfft(xs[0::2]), rfft(xs[1::2])
    out = [None] * (n // 2 + 1)
    out[0] = (even[0][0] + odd[0][0], None)
    out[n // 2] = (even[0][0] - odd[0][0], None)
    for k in range(1, n // 4):
        t = turned(odd[k], k, n)
        e = even[k]
        out[k] = (e[0] + t[0], e[1] + t[1])
        out[n // 2 - k] = (e[0] - t[0], t[1] - e[1])
    if n >= 4:
        k = n // 4
        out[k] = (even[k][0], -odd[k][0])
    return out


def irfft(zs):
    n = 2 * (len(zs) - 1)
    if n == 2:
        return [zs[0][0] + zs[1][0], zs[0][0] - zs[1][0]]
    even, odd = [None] * (n // 4 + 1), [None] * (n // 4 + 1)
    even[0] = (zs[0][0] + zs[n // 2][0], None)
    odd[0] = (zs[0][0] - zs[n // 2][0], None)
    for k in range(1, n // 4):
        a, b = zs[k], zs[n // 2 - k]
        even[k] = (a[0] + b[0], a[1] - b[1])
        odd[k] = turned((a[0] - b[0], a[1] + b[1]), n - k, n)
    k = n // 4
    even[k] = (zs[k][0].scale(2.0), None)
    odd[k] = (zs[k][1].scale(-2.0), None)
    xe, xo = irfft(even), irfft(odd)
    out = []
    for a, b in zip(xe, xo):
        out += [a, b]
    return out


R3 = math.sqrt(0.75)


def slow_forward(load):
    parts = []
    for a in range(3):
        parts.append(rfft([V(load((16 * a + 3 * b) % SLOW)) for b in range(16)]))
    out = [None] * HALF

    def put(c, d, z):
        k = next(k for k in range(SLOW) if k % 16 == c and k % 3 == d)
        if k <= SLOW // 2:
            out[k] = z
        elif out[SLOW - k] is None:
            out[SLOW - k] = (z[0], -z[1])

    for c in range(9):
        x, y, z = parts[0][c], parts[1][c], parts[2][c]
        if x[1] is None:
            t, s = y[0] + z[0], (y[0] - z[0]).scale(R3)
            put(c, 0, (x[0] + t, None))
            put(c, 1, (x[0] - t.scale(0.5), -s))
            continue
        tr, ti = y[0] + z[0], y[1] + z[1]
        sr, si = (y[0] - z[0]).scale(R3), (y[1] - z[1]).scale(R3)
        mr, mi = x[0] - tr.scale(0.5), x[1] - ti.scale(0.5)
        put(c, 0, (x[0] + tr, x[1] + ti))
        put(c, 1, (mr + si, mi - sr))
        put(c, 2, (mr - si, mi + sr))
    return out


def slow_inverse(bins):
    def get(c, d):
        k = next(k for k in range(SLOW) if k % 16 == c and k % 3 == d)
        if k <= SLOW // 2:
            return bins[k]
        z = bins[SLOW - k]
        return (z[0], -z[1])

    mid = [[None] * 9 for _ in range(3)]
    for c in range(9):
        x, y, z = get(c, 0), get(c, 1), get(c, 2)
        if c in (0, 8):
            tr, si = y[0], y[1].scale(2.0 * R3)
            m = x[0] - tr
            mid[0][c] = (x[0] + tr.scale(2.0), None)
            mid[1][c] = (m - si, None)
            mid[2][c] = (m + si, None)
            continue
        tr, ti = y[0] + z[0], y[1] + z[1]
        sr, si = (y[0] - z[0]).scale(R3), (y[1] - z[1]).scale(R3)
        mr, mi = x[0] - tr.scale(0.5), x[1] - ti.scale(0.5)
        mid[0][c] = (x[0] + tr, x[1] + ti)
        mid[1][c] = (mr - si, mi + sr)
        mid[2][c] = (mr + si, mi - sr)
    out = [None] * SLOW
    for a in range(3):
        xs = irfft(mid[a])
        for b in range(16):
            out[(16 * a + 3 * b) % SLOW] = xs[b]
    return out


def stack2(x):
    return jnp.concatenate([x, x], axis=0)


def put_split(hi_ref, lo_ref, k, re, im):
    rows = pl.ds(16 * k, 16)
    for half, x in ((0, re), (1, im)):
        hi = x.astype(jnp.bfloat16)
        lo = (x - hi.astype(jnp.float32)).astype(jnp.bfloat16)
        hi_ref[rows, pl.ds(FAST * half, FAST)] = hi
        lo_ref[rows, pl.ds(FAST * half, FAST)] = lo


def fast_dot(hi_ref, lo_ref, mat_ref, out_ref, pieces):
    step = ROWS // pieces
    for p in range(pieces):
        rows = pl.ds(p * step, step)
        hi, lo = hi_ref[rows, :], lo_ref[rows, :]
        mhi, mlo = mat_ref[0:256, :], mat_ref[256:512, :]
        acc = jnp.dot(hi, mhi, preferred_element_type=jnp.float32)
        acc = acc + jnp.dot(lo, mhi, preferred_element_type=jnp.float32)
        acc = acc + jnp.dot(hi, mlo, preferred_element_type=jnp.float32)
        out_ref[rows, :] = acc


def forward16(load, tw_ref, mat_ref, hi_ref, lo_ref, z_ref, pieces=1):
    bins = slow_forward(load)
    for k in range(HALF):
        re, im = bins[k]
        if k == 0:
            xr = re.get()
            put_split(hi_ref, lo_ref, 0, xr, jnp.zeros_like(xr))
            continue
        c, s = stack2(tw_ref[k, 0]), stack2(tw_ref[k, 1])
        if im is None:
            put_split(hi_ref, lo_ref, k, re.get() * c, -(re.get() * s))
            continue
        cr, ci = V(re.x * c, re.neg), V(im.x * c, im.neg)
        srr, sii = V(re.x * s, re.neg), V(im.x * s, im.neg)
        put_split(hi_ref, lo_ref, k, (cr + sii).get(), (ci - srr).get())
    fast_dot(hi_ref, lo_ref, mat_ref, z_ref, pieces)


def factors(z_ref, rows=16):
    def energy(k):
        re, im = z_ref[pl.ds(16 * k, 16), 0:128], z_ref[pl.ds(16 * k, 16), 128:256]
        return re * re + im * im

    def total(ks):
        es = [energy(k) for k in ks]
        while len(es) > 1:
            es = [es[i] + es[i + 1] if i + 1 < len(es) else es[i] for i in range(0, len(es), 2)]
        return es[0]

    low, high = total(range(1, 16)), total(range(17, 24))
    e16 = energy(16)
    lane = lax.broadcasted_iota(jnp.int32, (rows, FAST), 1)
    mirror = (FAST - 1) - lane

    def flip(x):
        return jnp.concatenate([
            jnp.take_along_axis(x[0:8], mirror[0:8], axis=1, mode="promise_in_bounds"),
            jnp.take_along_axis(x[8:16], mirror[8:16], axis=1, mode="promise_in_bounds"),
        ], axis=0)

    g0 = energy(0) + low
    g1 = e16 + high + energy(24) + flip(high)
    g2 = flip(low + e16)

    def nxt(x):
        return pltpu.roll(x, FAST - 1, 1)

    def prv(x):
        return pltpu.roll(x, 1, 1)

    g01, g12 = g0 + g1, g1 + g2
    g = g01 + g2
    ga = g + nxt(g0)
    gb_next, gb_prev = g12 + nxt(g01), g01 + prv(g12)
    gc = prv(g2) + g
    g0_at1 = prv(g) + g0
    g2_at2 = g2 + nxt(g)
    phase = lane % 4
    is0, is1, is2 = phase == 0, phase == 1, phase == 2
    l0 = jnp.where(is0, ga, jnp.where(is1, g0_at1, jnp.where(is2, gb_prev, gc)))
    l1 = jnp.where(is0, ga, jnp.where(is1, gb_next, jnp.where(is2, gb_prev, gc)))
    l2 = jnp.where(is0, ga, jnp.where(is1, gb_next, jnp.where(is2, g2_at2, gc)))
    f0, f1, f2 = [lax.rsqrt(l * np.float32(1.0 / 64) + np.float32(EPS)) for l in (l0, l1, l2)]
    return f0, f1, flip(f1), flip(f2)


def weights(fs, fx):
    p0, p1, q1, q2 = [a * b for a, b in zip(fs, fx)]
    return (p0, p0 + q2, p1 + q2, p1 + q1, p1)


def group_of(k):
    return 0 if k == 0 else 1 if k < 16 else 2 if k == 16 else 3 if k < 24 else 4


def cross_inverse(load_x, load_fx, load_s, load_fs, tw_ref, mat_ref, hi_ref, lo_ref, z_ref, store, pieces=1):
    hs = []
    for w in range(NWIN):
        fx = [stack2(f) for f in load_fx(w)]
        hs.append(weights(load_fs(w), fx))
    for k in range(HALF):
        cr = ci = None
        for w in range(NWIN):
            xr, xi = [stack2(x) for x in load_x(w, k)]
            sr, si = load_s(w, k)
            h = hs[w][group_of(k)]
            tr = (sr * xr + si * xi) * h
            ti = (si * xr - sr * xi) * h
            cr = tr if cr is None else cr + tr
            ci = ti if ci is None else ci + ti
        put_split(hi_ref, lo_ref, k, cr, ci)
    fast_dot(hi_ref, lo_ref, mat_ref, z_ref, pieces)
    bins = []
    for k in range(HALF):
        re, im = z_ref[pl.ds(16 * k, 16), 0:128], z_ref[pl.ds(16 * k, 16), 128:256]
        c, s = stack2(tw_ref[k, 2]), stack2(tw_ref[k, 3])
        real = re * c - im * s
        bins.append((V(real), None if k in (0, 24) else V(re * s + im * c)))
    for j, x in enumerate(slow_inverse(bins)):
        store(j, x.get())
def compute_kernel(x_ref, src_ref, fw_ref, iv_ref, tw_ref, out_ref, hi, lo, z, xs, fx, ss, fs, obuf, osem):
    def source_block(p, _):
        def load(n):
            return src_ref[pl.ds(pl.multiple_of(16 * p, 16), 16), pl.ds(FAST * n, FAST)].astype(jnp.float32)

        forward16(load, tw_ref, fw_ref, hi, lo, z)
        f = factors(z)
        for half in range(2):
            w = 2 * p + half
            for s in range(NSRC):
                row = 8 * half + s
                for i in range(4):
                    fs[w, s // 2, i, pl.ds(8 * (s % 2), 8), :] = jnp.broadcast_to(f[i][row : row + 1, :], (8, FAST))
                for k in range(HALF):
                    ss[w, s // 2, k, pl.ds(8 * (s % 2), 8), :] = jnp.broadcast_to(z[pl.ds(16 * k + row, 1), :], (8, 256))
        return 0

    lax.fori_loop(0, 2, source_block, 0)

    def keep(w, cb, half):
        for k in range(HALF):
            xs[w, cb, k] = z[pl.ds(16 * k + 8 * half, 8), :]

    def channel_block(i, _):
        w, p = i // 2, i % 2
        rows = pl.ds(pl.multiple_of(16 * p, 16), 16)

        def load(n):
            return x_ref[w, rows, pl.ds(FAST * n, FAST)].astype(jnp.float32)

        forward16(load, tw_ref, fw_ref, hi, lo, z)
        f = factors(z)
        for half in range(2):
            keep(w, 2 * p + half, half)
            for i in range(4):
                fx[w, 2 * p + half, i] = f[i][8 * half : 8 * half + 8, :]
        return 0

    lax.fori_loop(0, 8, channel_block, 0)

    def last_block(p, _):
        def load(n):
            return jnp.concatenate(
                [x_ref[2 * p + half, pl.ds(32, 8), pl.ds(FAST * n, FAST)].astype(jnp.float32) for half in range(2)], axis=0)

        forward16(load, tw_ref, fw_ref, hi, lo, z)
        f = factors(z)
        for half in range(2):
            keep(2 * p + half, 4, half)
            for i in range(4):
                fx[2 * p + half, 4, i] = f[i][8 * half : 8 * half + 8, :]
        return 0

    lax.fori_loop(0, 2, last_block, 0)

    def send(slot, cb, sp):
        return [pltpu.make_async_copy(
            obuf.at[slot, half],
            out_ref.at[2 * sp + half, pl.ds(pl.multiple_of(8 * cb, 8), 8), :],
            osem.at[slot, half]) for half in range(2)]

    def unit(u, _):
        cb, sp = u // 4, u % 4
        slot = u % 2

        @pl.when(u >= 2)
        def _():
            for c in send(slot, (u - 2) // 4, (u - 2) % 4):
                c.wait()

        def store(j, x):
            obuf[slot, 0, :, pl.ds(FAST * j, FAST)] = x[0:8]
            obuf[slot, 1, :, pl.ds(FAST * j, FAST)] = x[8:16]

        cross_inverse(
            lambda w, k: (xs[w, cb, k, :, 0:128], xs[w, cb, k, :, 128:256]),
            lambda w: [fx[w, cb, i] for i in range(4)],
            lambda w, k: (ss[w, sp, k, :, 0:128], ss[w, sp, k, :, 128:256]),
            lambda w: [fs[w, sp, i] for i in range(4)],
            tw_ref, iv_ref, hi, lo, z, store)
        for c in send(slot, cb, sp):
            c.start()
        return 0

    lax.fori_loop(0, 20, unit, 0)
    for u in (18, 19):
        for c in send(u % 2, u // 4, u % 4):
            c.wait()


def compute(x, src):
    fw, iv, tw = tables()
    vmem = pl.BlockSpec(memory_space=pltpu.VMEM)
    f32, bf16 = jnp.float32, jnp.bfloat16
    channels = x.shape[1]
    return pl.pallas_call(
        compute_kernel,
        out_shape=jax.ShapeDtypeStruct((NSRC, channels, NFFT), f32),
        in_specs=[vmem] * 5,
        out_specs=pl.BlockSpec(memory_space=pl.ANY),
        scratch_shapes=[
            pltpu.VMEM((ROWS, 256), bf16),
            pltpu.VMEM((ROWS, 256), bf16),
            pltpu.VMEM((ROWS, 256), f32),
            pltpu.VMEM((NWIN, 5, HALF, 8, 256), f32),
            pltpu.VMEM((NWIN, 5, 4, 8, FAST), f32),
            pltpu.VMEM((NWIN, 4, HALF, 16, 256), f32),
            pltpu.VMEM((NWIN, 4, 4, 16, FAST), f32),
            pltpu.VMEM((2, 2, 8, NFFT), f32),
            pltpu.SemaphoreType.DMA((2, 2)),
        ],
        compiler_params=pltpu.CompilerParams(vmem_limit_bytes=40 * 2**20),
    )(x, src, fw, iv, tw)


def shards(samples, source_ids):
    channels = samples.shape[2]
    section, line = lax.axis_index("rec"), lax.axis_index("ch")
    per_section = channels * 32
    ids = (jnp.arange(4, dtype=jnp.int32)[:, None] * per_section + line * channels + jnp.arange(channels, dtype=jnp.int32)[None, :]).reshape(-1)
    chooser = (source_ids[:, None] == ids[None, :]).astype(jnp.bfloat16)
    mine = jnp.dot(chooser, samples.reshape(4 * channels, NFFT), preferred_element_type=jnp.float32).astype(jnp.bfloat16)
    mine = lax.psum(mine, "ch")
    src = lax.all_gather(mine, "rec", axis=0).reshape(NWIN * NSRC, NFFT)
    x = lax.all_to_all(samples, "rec", split_axis=1, concat_axis=0, tiled=True)[:, 0]
    return compute(x, src)


def solution(mesh):
    return jax.shard_map(
        shards,
        mesh=mesh,
        in_specs=(P("rec", None, "ch", None), P()),
        out_specs=P(None, ("rec", "ch"), None),
        check_vma=False,
    )
```

time: 574 us -> 375 us (0.65)
  matrix products: 223 us -> 2.66 us
  waiting for transfers between devices: 175 us -> 307 us
  local copies, waits for them, and re-layouts: 97.9 us -> 0.1 us
  other arithmetic: 54.5 us -> 0.08 us
  Pallas kernels: 0 us -> 23.3 us
  blocking collectives: 0 us -> 22.6 us
    dot_general x14 -> x1, matrix products: 223 us -> 2.66 us  [shards(): jnp.dot(chooser, samples.reshape(4 * channels, NFFT), preferred_element_t...]
    psum x1, waiting for transfers between devices: 152 us -> 307 us  [shards(): mine = lax.psum(mine, 'ch')]
    reshape x6 -> x0, local copies, waits for them, and re-layouts: 57.3 us -> none  [the longest x2 22.8 us: transform(): shaped = real_part.reshape(leading + (inner_size, outer_size))]
    sub x4 -> x0, other arithmetic: 39.5 us -> none  [accumulate(): cross_imag = cross_imag + left_imag * right_real - left_real * right_imag]
    pallas_call x0 -> x1, Pallas kernels: none -> 23.3 us  [compute(): pl.pallas_call(compute_kernel, out_shape=jax.ShapeDtypeStruct((NSRC, chan...]
    all_to_all x1, waiting for transfers between devices: 23.3 us -> 0.01 us  [shards(): lax.all_to_all(samples, 'rec', split_axis=1, concat_axis=0, tiled=True)]
    all_gather x0 -> x1, blocking collectives: none -> 22.6 us  [shards(): src = lax.all_gather(mine, 'rec', axis=0).reshape(NWIN * NSRC, NFFT)]
    mul x9 -> x0, local copies, waits for them, and re-layouts: 19.7 us -> none  [the longest x8 10.8 us: accumulate(): cross_real = cross_real + left_real * right_real + left_imag * right_imag]
  transfers between devices with their start and end apart: 2 -> 2, of which waited for: 2 -> 1; matrix products, arithmetic and copies ran while one was open for 0% -> 1% of each run, Pallas kernels for 0% -> 0%
where the time goes in v1:
time: 375 us; the launch traced here: 374 us
  waiting for transfers between devices  307 us (82%)
  Pallas kernels  23.3 us (6%)
  blocking collectives  22.6 us (6%)
  between operations  13.4 us (4%)
  starting transfers between devices  5.15 us (1%)
    psum x1, waiting for transfers between devices, shards(): mine = lax.psum(mine, 'ch')  307 us
    pallas_call x1, Pallas kernels, compute(): pl.pallas_call(compute_kernel, out_shape=jax.ShapeDtypeStruct((NSRC, chan...  23.3 us
    all_gather x1, blocking collectives, shards(): src = lax.all_gather(mine, 'rec', axis=0).reshape(NWIN * NSRC, NFFT)  22.6 us
  transfers between devices with their start and end apart: 2, of which 1 were waited for; matrix products, arithmetic and copies ran while one was open for 1% of the time, Pallas kernels for 0%

profile of v1, /device:TPU:1, one launch (start us, length us, event | category | flops | bytes accessed | tf_op | source)
XLA Modules:
  0.0 374.4 jit_solution(4126631068384993697)
XLA Ops:
  6.5 0.0 copy-start.3
  6.5 5.1 %all-to-all-start = ((bf16[1,4,40,6144]{3,2,0,1:T(8,128)(2,1)}), bf16[1,4,40,6144]{3,2,0,1:T(8,128)(2,1)S(1)}, u32[]{:S(2)}, u32[]{:S(2)}) async-start(bf16[1,4,40,6144]{3,2,0,1:T(8,128)(2,1)} %bitcast.9), calls=%async_computation | async-start | bytes 3932160 | tf_op jit(solution)/shard_map/all_to_all | solution.py:441
  11.7 0.0 copy-start
  11.7 0.0 copy-start.1
  11.7 0.0 copy-start.2
  11.7 0.0 all-reduce.2.cloned.1.call-start
  11.7 0.1 iota_add_fusion
  11.8 0.1 add.38
  11.9 0.0 copy-done.3
  11.9 2.7 fusion
  14.5 0.0 all-reduce.2.cloned.1.call-update
  14.6 307.0 %all-reduce.2.cloned.1.call-done = bf16[1,8,6144]{2,1,0:T(8,128)(2,1)} async-done(((bf16[1,8,6144]{2,1,0:T(8,128)(2,1)}), bf16[1,8,6144]{2,1,0:T(8,128)(2,1)}) %all-reduce.2.cloned.1.call-update) | async-done | bytes 98320 | tf_op jit(solution)/shard_map/psum | solution.py:439
  321.5 22.6 %all_gather.7 = bf16[4,8,6144]{2,1,0:T(8,128)(2,1)S(1)} all-gather(bf16[1,8,6144]{2,1,0:T(8,128)(2,1)} %all-reduce.2.cloned.1.call-done), channel_id=1, replica_groups=mesh['rec'=4,'ch'=32] {'rec'}, dimensions={0}, use_global_device_ids=true | all-gather | bytes 491520 | tf_op jit(solution)/shard_map/all_gather | solution.py:440
  344.2 0.0 all-to-all-done
  344.2 0.0 copy-done
  344.2 0.0 copy-done.1
  344.2 0.0 copy-done.2
  344.2 23.3 %shard_map.55 = f32[8,40,6144]{2,1,0:T(8,128)} custom-call(bf16[4,40,6144]{2,1,0:T(8,128)(2,1)S(1)} %bitcast.7, bf16[32,6144]{1,0:T(8,128)(2,1)S(1)} %bitcast.8, bf16[512,256]{1,0:T(8,128)(2,1)S(1)} %copy-done.2, bf16[512,256]{1,0:T(8,128)(2,1)S(1)} %copy-done.1, f32[25,4,8,128]{3,2,1,0:T(8,128)S(1)} %copy-done), custom_call_target="tpu_custom_call" | custom-call | tf_op jit(solution)/shard_map/pallas_call | solution.py:412
  (1 shorter events, 0.0 us)
Async XLA Ops:
  6.5 5.3 %copy-start.3 = (s32[8]{0:T(128)S(1)}, s32[8]{0:T(128)}, u32[]{:S(2)}) copy-start(s32[8]{0:T(128)} %param.6) | copy-start | bytes 100
  6.5 337.7 %all-to-all-start = ((bf16[1,4,40,6144]{3,2,0,1:T(8,128)(2,1)}), bf16[1,4,40,6144]{3,2,0,1:T(8,128)(2,1)S(1)}, u32[]{:S(2)}, u32[]{:S(2)}) async-start(bf16[1,4,40,6144]{3,2,0,1:T(8,128)(2,1)} %bitcast.9), calls=%async_computation | async-start | bytes 3932160 | tf_op jit(solution)/shard_map/all_to_all | solution.py:441
  11.7 332.5 %copy-start = (f32[25,4,8,128]{3,2,1,0:T(8,128)S(1)}, f32[25,4,8,128]{3,2,1,0:T(8,128)}, u32[]{:S(2)}) copy-start(f32[25,4,8,128]{3,2,1,0:T(8,128)} %constant.16.clone.tw_ref) | copy-start | bytes 1228804
  11.7 332.5 %copy-start.1 = (bf16[512,256]{1,0:T(8,128)(2,1)S(1)}, bf16[512,256]{1,0:T(8,128)(2,1)}, u32[]{:S(2)}) copy-start(bf16[512,256]{1,0:T(8,128)(2,1)} %constant.15.clone.iv_ref) | copy-start | bytes 786436
  11.7 332.5 %copy-start.2 = (bf16[512,256]{1,0:T(8,128)(2,1)S(1)}, bf16[512,256]{1,0:T(8,128)(2,1)}, u32[]{:S(2)}) copy-start(bf16[512,256]{1,0:T(8,128)(2,1)} %constant.14.clone.fw_ref) | copy-start | bytes 786436
  11.7 309.9 %all-reduce.2.cloned.1.call-start = ((), (), s32[]{:S(2)}) async-start(), calls=%async_computation.1 | async-start | bytes 196608 | tf_op jit(solution)/shard_map/psum | solution.py:439
Sparse Core Ops, SparseCore 0:
  15.0 306.5 all-reduce.1

commit v2 on v1

--- a/solution.py
+++ b/solution.py
@@ -193,43 +193,36 @@
     return jnp.concatenate([x, x], axis=0)
 
 
-def put_split(hi_ref, lo_ref, k, re, im):
+def put(y_ref, k, re, im):
     rows = pl.ds(16 * k, 16)
-    for half, x in ((0, re), (1, im)):
-        hi = x.astype(jnp.bfloat16)
-        lo = (x - hi.astype(jnp.float32)).astype(jnp.bfloat16)
-        hi_ref[rows, pl.ds(FAST * half, FAST)] = hi
-        lo_ref[rows, pl.ds(FAST * half, FAST)] = lo
-
-
-def fast_dot(hi_ref, lo_ref, mat_ref, out_ref, pieces):
-    step = ROWS // pieces
-    for p in range(pieces):
-        rows = pl.ds(p * step, step)
-        hi, lo = hi_ref[rows, :], lo_ref[rows, :]
-        mhi, mlo = mat_ref[0:256, :], mat_ref[256:512, :]
-        acc = jnp.dot(hi, mhi, preferred_element_type=jnp.float32)
-        acc = acc + jnp.dot(lo, mhi, preferred_element_type=jnp.float32)
-        acc = acc + jnp.dot(hi, mlo, preferred_element_type=jnp.float32)
-        out_ref[rows, :] = acc
-
-
-def forward16(load, tw_ref, mat_ref, hi_ref, lo_ref, z_ref, pieces=1):
+    y_ref[rows, 0:128] = re
+    y_ref[rows, 128:256] = im
+
+
+def fast_dot(y_ref, mat_ref, out_ref):
+    y = y_ref[...]
+    hi = y.astype(jnp.bfloat16)
+    lo = (y - hi.astype(jnp.float32)).astype(jnp.bfloat16)
+    mats = jnp.concatenate([mat_ref[0:256, :], mat_ref[...]], axis=0)
+    out_ref[...] = jnp.dot(jnp.concatenate([hi, lo, hi], axis=1), mats, preferred_element_type=jnp.float32)
+
+
+def forward16(load, tw_ref, mat_ref, y_ref, z_ref):
     bins = slow_forward(load)
     for k in range(HALF):
         re, im = bins[k]
         if k == 0:
             xr = re.get()
-            put_split(hi_ref, lo_ref, 0, xr, jnp.zeros_like(xr))
+            put(y_ref, 0, xr, jnp.zeros_like(xr))
             continue
         c, s = stack2(tw_ref[k, 0]), stack2(tw_ref[k, 1])
         if im is None:
-            put_split(hi_ref, lo_ref, k, re.get() * c, -(re.get() * s))
+            put(y_ref, k, re.get() * c, -(re.get() * s))
             continue
         cr, ci = V(re.x * c, re.neg), V(im.x * c, im.neg)
         srr, sii = V(re.x * s, re.neg), V(im.x * s, im.neg)
-        put_split(hi_ref, lo_ref, k, (cr + sii).get(), (ci - srr).get())
-    fast_dot(hi_ref, lo_ref, mat_ref, z_ref, pieces)
+        put(y_ref, k, (cr + sii).get(), (ci - srr).get())
+    fast_dot(y_ref, mat_ref, z_ref)
 
 
 def factors(z_ref, rows=16):
@@ -289,7 +282,7 @@
     return 0 if k == 0 else 1 if k < 16 else 2 if k == 16 else 3 if k < 24 else 4
 
 
-def cross_inverse(load_x, load_fx, load_s, load_fs, tw_ref, mat_ref, hi_ref, lo_ref, z_ref, store, pieces=1):
+def cross_inverse(load_x, load_fx, load_s, load_fs, tw_ref, mat_ref, y_ref, z_ref, store):
     hs = []
     for w in range(NWIN):
         fx = [stack2(f) for f in load_fx(w)]
@@ -304,8 +297,8 @@
             ti = (si * xr - sr * xi) * h
             cr = tr if cr is None else cr + tr
             ci = ti if ci is None else ci + ti
-        put_split(hi_ref, lo_ref, k, cr, ci)
-    fast_dot(hi_ref, lo_ref, mat_ref, z_ref, pieces)
+        put(y_ref, k, cr, ci)
+    fast_dot(y_ref, mat_ref, z_ref)
     bins = []
     for k in range(HALF):
         re, im = z_ref[pl.ds(16 * k, 16), 0:128], z_ref[pl.ds(16 * k, 16), 128:256]
@@ -314,60 +307,154 @@
         bins.append((V(real), None if k in (0, 24) else V(re * s + im * c)))
     for j, x in enumerate(slow_inverse(bins)):
         store(j, x.get())
-def compute_kernel(x_ref, src_ref, fw_ref, iv_ref, tw_ref, out_ref, hi, lo, z, xs, fx, ss, fs, obuf, osem):
-    def source_block(p, _):
-        def load(n):
-            return src_ref[pl.ds(pl.multiple_of(16 * p, 16), 16), pl.ds(FAST * n, FAST)].astype(jnp.float32)
-
-        forward16(load, tw_ref, fw_ref, hi, lo, z)
-        f = factors(z)
-        for half in range(2):
-            w = 2 * p + half
-            for s in range(NSRC):
-                row = 8 * half + s
-                for i in range(4):
-                    fs[w, s // 2, i, pl.ds(8 * (s % 2), 8), :] = jnp.broadcast_to(f[i][row : row + 1, :], (8, FAST))
-                for k in range(HALF):
-                    ss[w, s // 2, k, pl.ds(8 * (s % 2), 8), :] = jnp.broadcast_to(z[pl.ds(16 * k + row, 1), :], (8, 256))
-        return 0
-
-    lax.fori_loop(0, 2, source_block, 0)
+GROUP = 16
+LINE = 8
+PIECE = NFFT // GROUP
+CHUNKS = ((0, 16), (16, 16), (32, 8))
+MESH = pl.DeviceIdType.MESH
+
+
+def kernel(ids_ref, x_ref, flat_ref, fw_ref, iv_ref, tw_ref, out_ref,
+           y, z, flat, recvx, part, recv1, recv2, srcs, xs, fx, ss, fs, obuf,
+           flat_sem, own_sem, send_x, recv_x, send1, got1, send2, got2, send3, got3, osem):
+    rec, ch = lax.axis_index("rec"), lax.axis_index("ch")
+    q, x_hi = ch // 2, ch % 2
+    line = x_hi * 4 + rec
+    pair = rec // 2
+    sibling = rec + 1 - 2 * (rec % 2)
+    far = [(rec + 2) % 4, (sibling + 2) % 4]
+    q_peer = [(q + i) % GROUP for i in range(1, GROUP)]
+    q_id = [(rec, p * 2 + x_hi) for p in q_peer]
+    l_peer = [(line + i) % LINE for i in range(1, LINE)]
+    l_id = [(p % 4, q * 2 + p // 4) for p in l_peer]
+
+    load_flat = pltpu.make_async_copy(flat_ref, flat, flat_sem)
+    load_own = pltpu.make_async_copy(x_ref.at[rec], recvx.at[rec], own_sem)
+    load_flat.start()
+    load_own.start()
+    barrier = pltpu.get_barrier_semaphore()
+    for d in q_id + l_id:
+        pl.semaphore_signal(barrier, inc=1, device_id=d, device_id_type=MESH)
+
+    def move_x(n, peer, start, rows):
+        return pltpu.make_async_remote_copy(
+            src_ref=x_ref.at[peer, pl.ds(start, rows), :], dst_ref=recvx.at[rec, pl.ds(start, rows), :],
+            send_sem=send_x.at[n], recv_sem=recv_x.at[n], device_id=(peer, ch), device_id_type=MESH)
+
+    moves = []
+    for c, (start, rows) in enumerate(CHUNKS):
+        moves.append([move_x(2 * c + i, far[i], start, rows) for i in range(2)])
+    near = move_x(6, sibling, 0, 40)
+
+    row = lax.broadcasted_iota(jnp.int32, (NSRC, 160), 0)
+    col = lax.broadcasted_iota(jnp.int32, (NSRC, 160), 1)
+    ids = jnp.zeros((NSRC, 160), jnp.int32)
+    for s in range(NSRC):
+        ids = jnp.where(row == s, ids_ref[s], ids)
+    here = (col // 40) * 1280 + ch * 40 + col % 40
+    chooser = jnp.where(ids == here, 1.0, 0.0).astype(jnp.bfloat16)
+    load_flat.wait()
+    for j in range(GROUP):
+        part[j] = jnp.dot(chooser, flat[:, pl.ds(PIECE * j, PIECE)], preferred_element_type=jnp.float32)
+    recv1[q] = part[q]
+
+    pl.semaphore_wait(barrier, GROUP - 1 + LINE - 1)
+
+    for m in moves[0]:
+        m.start()
+    step1 = [pltpu.make_async_remote_copy(
+        src_ref=part.at[p], dst_ref=recv1.at[q], send_sem=send1.at[i], recv_sem=got1.at[i],
+        device_id=d, device_id_type=MESH) for i, (p, d) in enumerate(zip(q_peer, q_id))]
+    for m in step1:
+        m.start()
+    near.start()
+    for m in moves[1] + moves[2]:
+        m.start()
 
     def keep(w, cb, half):
         for k in range(HALF):
             xs[w, cb, k] = z[pl.ds(16 * k + 8 * half, 8), :]
 
-    def channel_block(i, _):
-        w, p = i // 2, i % 2
+    def whole_block(w, p):
         rows = pl.ds(pl.multiple_of(16 * p, 16), 16)
-
-        def load(n):
-            return x_ref[w, rows, pl.ds(FAST * n, FAST)].astype(jnp.float32)
-
-        forward16(load, tw_ref, fw_ref, hi, lo, z)
+        forward16(lambda n: recvx[w, rows, pl.ds(FAST * n, FAST)].astype(jnp.float32), tw_ref, fw_ref, y, z)
         f = factors(z)
         for half in range(2):
             keep(w, 2 * p + half, half)
             for i in range(4):
                 fx[w, 2 * p + half, i] = f[i][8 * half : 8 * half + 8, :]
-        return 0
-
-    lax.fori_loop(0, 8, channel_block, 0)
-
-    def last_block(p, _):
+
+    def half_block(first):
         def load(n):
             return jnp.concatenate(
-                [x_ref[2 * p + half, pl.ds(32, 8), pl.ds(FAST * n, FAST)].astype(jnp.float32) for half in range(2)], axis=0)
-
-        forward16(load, tw_ref, fw_ref, hi, lo, z)
+                [recvx[first + half, pl.ds(32, 8), pl.ds(FAST * n, FAST)].astype(jnp.float32) for half in range(2)], axis=0)
+
+        forward16(load, tw_ref, fw_ref, y, z)
         f = factors(z)
         for half in range(2):
-            keep(2 * p + half, 4, half)
+            keep(first + half, 4, half)
             for i in range(4):
-                fx[2 * p + half, 4, i] = f[i][8 * half : 8 * half + 8, :]
+                fx[first + half, 4, i] = f[i][8 * half : 8 * half + 8, :]
+
+    load_own.wait()
+
+    def own(p, _):
+        whole_block(rec, p)
         return 0
 
-    lax.fori_loop(0, 2, last_block, 0)
+    lax.fori_loop(0, 2, own, 0)
+
+    for m in step1:
+        m.wait()
+    total = recv1[0]
+    for j in range(1, GROUP):
+        total = total + recv1[j]
+    recv2[line] = total
+    step2 = [pltpu.make_async_remote_copy(
+        src_ref=recv2.at[line], dst_ref=recv2.at[line], send_sem=send2.at[i], recv_sem=got2.at[i],
+        device_id=d, device_id_type=MESH) for i, d in enumerate(l_id)]
+    for m in step2:
+        m.start()
+
+    near.wait()
+
+    def second(p, _):
+        whole_block(sibling, p)
+        return 0
+
+    lax.fori_loop(0, 2, second, 0)
+
+    for m in step2:
+        m.wait()
+    srcs[q] = jnp.concatenate([recv2[w] + recv2[4 + w] for w in range(NWIN)], axis=0).astype(jnp.bfloat16)
+    step3 = [pltpu.make_async_remote_copy(
+        src_ref=srcs.at[q], dst_ref=srcs.at[q], send_sem=send3.at[i], recv_sem=got3.at[i],
+        device_id=d, device_id_type=MESH) for i, d in enumerate(q_id)]
+    for m in step3:
+        m.start()
+    half_block(2 * pair)
+    for m in step3:
+        m.wait()
+
+    def source_block(p, _):
+        rows = pl.ds(pl.multiple_of(16 * p, 16), 16)
+
+        def load(n):
+            return srcs[n // 3, rows, pl.ds(FAST * (n % 3), FAST)].astype(jnp.float32)
+
+        forward16(load, tw_ref, fw_ref, y, z)
+        f = factors(z)
+        for half in range(2):
+            w = 2 * p + half
+            for s in range(NSRC):
+                r = 8 * half + s
+                for i in range(4):
+                    fs[w, s // 2, i, pl.ds(8 * (s % 2), 8), :] = jnp.broadcast_to(f[i][r : r + 1, :], (8, FAST))
+                for k in range(HALF):
+                    ss[w, s // 2, k, pl.ds(8 * (s % 2), 8), :] = jnp.broadcast_to(z[pl.ds(16 * k + r, 1), :], (8, 256))
+        return 0
+
+    lax.fori_loop(0, 2, source_block, 0)
 
     def send(slot, cb, sp):
         return [pltpu.make_async_copy(
@@ -393,53 +480,63 @@
             lambda w: [fx[w, cb, i] for i in range(4)],
             lambda w, k: (ss[w, sp, k, :, 0:128], ss[w, sp, k, :, 128:256]),
             lambda w: [fs[w, sp, i] for i in range(4)],
-            tw_ref, iv_ref, hi, lo, z, store)
+            tw_ref, iv_ref, y, z, store)
         for c in send(slot, cb, sp):
             c.start()
         return 0
 
-    lax.fori_loop(0, 20, unit, 0)
+    for c in range(2):
+        for m in moves[c]:
+            m.wait()
+
+        def two(i, _):
+            whole_block(2 * (1 - pair) + i, c)
+            return 0
+
+        lax.fori_loop(0, 2, two, 0)
+        lax.fori_loop(8 * c, 8 * c + 8, unit, 0)
+
+    for m in moves[2]:
+        m.wait()
+    half_block(2 * (1 - pair))
+    lax.fori_loop(16, 20, unit, 0)
     for u in (18, 19):
         for c in send(u % 2, u // 4, u % 4):
             c.wait()
 
 
-def compute(x, src):
+def shards(samples, source_ids):
     fw, iv, tw = tables()
+    channels = samples.shape[2]
     vmem = pl.BlockSpec(memory_space=pltpu.VMEM)
+    anywhere = pl.BlockSpec(memory_space=pl.ANY)
     f32, bf16 = jnp.float32, jnp.bfloat16
-    channels = x.shape[1]
+    dma = pltpu.SemaphoreType.DMA
     return pl.pallas_call(
-        compute_kernel,
+        kernel,
         out_shape=jax.ShapeDtypeStruct((NSRC, channels, NFFT), f32),
-        in_specs=[vmem] * 5,
-        out_specs=pl.BlockSpec(memory_space=pl.ANY),
+        in_specs=[pl.BlockSpec(memory_space=pltpu.SMEM), anywhere, anywhere, vmem, vmem, vmem],
+        out_specs=anywhere,
         scratch_shapes=[
-            pltpu.VMEM((ROWS, 256), bf16),
-            pltpu.VMEM((ROWS, 256), bf16),
             pltpu.VMEM((ROWS, 256), f32),
+            pltpu.VMEM((ROWS, 256), f32),
+            pltpu.VMEM((4 * channels, NFFT), bf16),
+            pltpu.VMEM((NWIN, channels, NFFT), bf16),
+            pltpu.VMEM((GROUP, NSRC, PIECE), f32),
+            pltpu.VMEM((GROUP, NSRC, PIECE), f32),
+            pltpu.VMEM((LINE, NSRC, PIECE), f32),
+            pltpu.VMEM((GROUP, NWIN * NSRC, PIECE), bf16),
             pltpu.VMEM((NWIN, 5, HALF, 8, 256), f32),
             pltpu.VMEM((NWIN, 5, 4, 8, FAST), f32),
             pltpu.VMEM((NWIN, 4, HALF, 16, 256), f32),
             pltpu.VMEM((NWIN, 4, 4, 16, FAST), f32),
             pltpu.VMEM((2, 2, 8, NFFT), f32),
-            pltpu.SemaphoreType.DMA((2, 2)),
+            dma, dma, dma((7,)), dma((7,)), dma((15,)), dma((15,)), dma((7,)), dma((7,)), dma((15,)), dma((15,)),
+            dma((2, 2)),
         ],
-        compiler_params=pltpu.CompilerParams(vmem_limit_bytes=40 * 2**20),
-    )(x, src, fw, iv, tw)
-
-
-def shards(samples, source_ids):
-    channels = samples.shape[2]
-    section, line = lax.axis_index("rec"), lax.axis_index("ch")
-    per_section = channels * 32
-    ids = (jnp.arange(4, dtype=jnp.int32)[:, None] * per_section + line * channels + jnp.arange(channels, dtype=jnp.int32)[None, :]).reshape(-1)
-    chooser = (source_ids[:, None] == ids[None, :]).astype(jnp.bfloat16)
-    mine = jnp.dot(chooser, samples.reshape(4 * channels, NFFT), preferred_element_type=jnp.float32).astype(jnp.bfloat16)
-    mine = lax.psum(mine, "ch")
-    src = lax.all_gather(mine, "rec", axis=0).reshape(NWIN * NSRC, NFFT)
-    x = lax.all_to_all(samples, "rec", split_axis=1, concat_axis=0, tiled=True)[:, 0]
-    return compute(x, src)
+        compiler_params=pltpu.CompilerParams(
+            collective_id=0, has_side_effects=True, vmem_limit_bytes=48 * 2**20),
+    )(source_ids, samples[0], samples.reshape(4 * channels, NFFT), fw, iv, tw)
 
 
 def solution(mesh):

time: 375 us -> 71.9 us (0.19)
  waiting for transfers between devices: 307 us -> 0 us
  Pallas kernels: 23.3 us -> 59.1 us
  blocking collectives: 22.6 us -> 0 us
  between operations: 13.4 us -> 0.01 us
  local copies, waits for them, and re-layouts: 0.1 us -> 12.5 us
  starting transfers between devices: 5.15 us -> 0 us
    psum x1 -> x0, waiting for transfers between devices: 307 us -> none  [shards(): mine = lax.psum(mine, 'ch')]
    pallas_call x1, Pallas kernels: 23.3 us -> 59.1 us  [shards(): pl.pallas_call(kernel, out_shape=jax.ShapeDtypeStruct((NSRC, channels, NF...]
    all_gather x1 -> x0, blocking collectives: 22.6 us -> none  [shards(): src = lax.all_gather(mine, 'rec', axis=0).reshape(NWIN * NSRC, NFFT)]
    unnamed x8 -> x11, local copies, waits for them, and re-layouts: 0.01 us -> 12.5 us
    all_to_all x1 -> x0, starting transfers between devices: 5.12 us -> none  [shards(): lax.all_to_all(samples, 'rec', split_axis=1, concat_axis=0, tiled=True)]
  transfers between devices with their start and end apart: 2 -> 0, of which waited for: 1 -> 0; matrix products, arithmetic and copies ran while one was open for 1% -> 0% of each run, Pallas kernels for 0% -> 0%
where the time goes in v2:
time: 71.9 us; the launch traced here: 71.6 us
  Pallas kernels  59.1 us (82%)
  local copies, waits for them, and re-layouts  12.5 us (17%)
    pallas_call x1, Pallas kernels, shards(): pl.pallas_call(kernel, out_shape=jax.ShapeDtypeStruct((NSRC, channels, NF...  59.1 us
    unnamed x11, local copies, waits for them, and re-layouts  12.5 us

profile of v2, /device:TPU:1, one launch (start us, length us, event | category | flops | bytes accessed | tf_op | source)
XLA Modules:
  0.0 71.6 jit_solution(13343002559154161298)
XLA Ops:
  0.0 0.0 copy-start
  0.0 1.5 %copy-done = bf16[1,4,40,6144]{3,2,1,0:T(8,128)(2,1)S(1)} copy-done((bf16[1,4,40,6144]{3,2,1,0:T(8,128)(2,1)S(1)}, bf16[1,4,40,6144]{3,2,1,0:T(8,128)(2,1)}, u32[]{:S(2)}) %copy-start) | copy-done | bytes 1966104
  1.5 0.0 copy-start.1
  1.5 1.0 %copy-done.1 = f32[25,4,8,128]{3,2,1,0:T(8,128)S(1)} copy-done((f32[25,4,8,128]{3,2,1,0:T(8,128)S(1)}, f32[25,4,8,128]{3,2,1,0:T(8,128)}, u32[]{:S(2)}) %copy-start.1) | copy-done | bytes 409624
  2.5 0.0 copy-start.2
  2.6 0.9 %copy-done.2 = bf16[512,256]{1,0:T(8,128)(2,1)S(1)} copy-done((bf16[512,256]{1,0:T(8,128)(2,1)S(1)}, bf16[512,256]{1,0:T(8,128)(2,1)}, u32[]{:S(2)}) %copy-start.2) | copy-done | bytes 262168
  3.5 0.0 copy-start.3
  3.5 0.9 %copy-done.3 = bf16[512,256]{1,0:T(8,128)(2,1)S(1)} copy-done((bf16[512,256]{1,0:T(8,128)(2,1)S(1)}, bf16[512,256]{1,0:T(8,128)(2,1)}, u32[]{:S(2)}) %copy-start.3) | copy-done | bytes 262168
  4.4 0.0 copy-start.4
  4.5 0.7 copy-done.4
  5.1 59.1 %shard_map.55 = f32[8,40,6144]{2,1,0:T(8,128)} custom-call(s32[8]{0:T(128)S(1)} %copy-done.4, bf16[4,40,6144]{2,1,0:T(8,128)(2,1)S(1)} %bitcast.2, bf16[160,6144]{1,0:T(8,128)(2,1)S(1)} %bitcast.3, bf16[512,256]{1,0:T(8,128)(2,1)S(1)} %copy-done.3, bf16[512,256]{1,0:T(8,128)(2,1)S(1)} %copy-done.2, f32[25,4,8,128]{3,2,1,0:T(8,128)S(1)} %copy-done.1), custom_call_target="tpu_custom_call" | custom-call | tf_op jit(solution)/shard_map/pallas_call | solution.py:515
  64.2 7.4 %copy.7 = f32[8,40,6144]{2,1,0:T(8,128)} copy(f32[8,40,6144]{2,1,0:T(8,128)} %shard_map.55) | data formatting | bytes 15728640
Async XLA Ops:
  0.0 1.5 %copy-start = (bf16[1,4,40,6144]{3,2,1,0:T(8,128)(2,1)S(1)}, bf16[1,4,40,6144]{3,2,1,0:T(8,128)(2,1)}, u32[]{:S(2)}) copy-start(bf16[1,4,40,6144]{3,2,1,0:T(8,128)(2,1)} %param.5) | copy-start | bytes 5898244
  1.5 1.0 %copy-start.1 = (f32[25,4,8,128]{3,2,1,0:T(8,128)S(1)}, f32[25,4,8,128]{3,2,1,0:T(8,128)}, u32[]{:S(2)}) copy-start(f32[25,4,8,128]{3,2,1,0:T(8,128)} %constant.8.clone.tw_ref) | copy-start | bytes 1228804
  2.5 0.9 %copy-start.2 = (bf16[512,256]{1,0:T(8,128)(2,1)S(1)}, bf16[512,256]{1,0:T(8,128)(2,1)}, u32[]{:S(2)}) copy-start(bf16[512,256]{1,0:T(8,128)(2,1)} %constant.7.clone.iv_ref) | copy-start | bytes 786436
  3.5 0.9 %copy-start.3 = (bf16[512,256]{1,0:T(8,128)(2,1)S(1)}, bf16[512,256]{1,0:T(8,128)(2,1)}, u32[]{:S(2)}) copy-start(bf16[512,256]{1,0:T(8,128)(2,1)} %constant.6.clone.fw_ref) | copy-start | bytes 786436
  4.4 0.7 copy-start.4

commit v3 on v2

--- a/solution.py
+++ b/solution.py
@@ -302,7 +302,7 @@
     bins = []
     for k in range(HALF):
         re, im = z_ref[pl.ds(16 * k, 16), 0:128], z_ref[pl.ds(16 * k, 16), 128:256]
-        c, s = stack2(tw_ref[k, 2]), stack2(tw_ref[k, 3])
+        c, s = stack2(tw_ref[k, 0]), stack2(tw_ref[k, 1])
         real = re * c - im * s
         bins.append((V(real), None if k in (0, 24) else V(re * s + im * c)))
     for j, x in enumerate(slow_inverse(bins)):
@@ -314,9 +314,9 @@
 MESH = pl.DeviceIdType.MESH
 
 
-def kernel(ids_ref, x_ref, flat_ref, fw_ref, iv_ref, tw_ref, out_ref,
-           y, z, flat, recvx, part, recv1, recv2, srcs, xs, fx, ss, fs, obuf,
-           flat_sem, own_sem, send_x, recv_x, send1, got1, send2, got2, send3, got3, osem):
+def gather_kernel(ids_hbm, x_ref, flat_ref, fw_hbm, tw_hbm, iv_hbm, it_hbm, xs, fx, ss, fs, iv_ref, it_ref,
+                  ids_ref, fw_ref, tw_ref, y, z, flat, recvx, part, recv1, recv2, srcs,
+                  load_sem, flat_sem, own_sem, send_x, recv_x, send1, got1, send2, got2, send3, got3):
     rec, ch = lax.axis_index("rec"), lax.axis_index("ch")
     q, x_hi = ch // 2, ch % 2
     line = x_hi * 4 + rec
@@ -328,10 +328,15 @@
     l_peer = [(line + i) % LINE for i in range(1, LINE)]
     l_id = [(p % 4, q * 2 + p // 4) for p in l_peer]
 
+    load_ids = pltpu.make_async_copy(ids_hbm, ids_ref, load_sem.at[0])
     load_flat = pltpu.make_async_copy(flat_ref, flat, flat_sem)
+    load_fw = pltpu.make_async_copy(fw_hbm, fw_ref, load_sem.at[1])
+    load_tw = pltpu.make_async_copy(tw_hbm, tw_ref, load_sem.at[2])
     load_own = pltpu.make_async_copy(x_ref.at[rec], recvx.at[rec], own_sem)
-    load_flat.start()
-    load_own.start()
+    load_iv = pltpu.make_async_copy(iv_hbm, iv_ref, load_sem.at[3])
+    load_it = pltpu.make_async_copy(it_hbm, it_ref, load_sem.at[4])
+    for m in (load_ids, load_flat, load_fw, load_tw, load_own, load_iv, load_it):
+        m.start()
     barrier = pltpu.get_barrier_semaphore()
     for d in q_id + l_id:
         pl.semaphore_signal(barrier, inc=1, device_id=d, device_id_type=MESH)
@@ -346,6 +351,7 @@
         moves.append([move_x(2 * c + i, far[i], start, rows) for i in range(2)])
     near = move_x(6, sibling, 0, 40)
 
+    load_ids.wait()
     row = lax.broadcasted_iota(jnp.int32, (NSRC, 160), 0)
     col = lax.broadcasted_iota(jnp.int32, (NSRC, 160), 1)
     ids = jnp.zeros((NSRC, 160), jnp.int32)
@@ -368,8 +374,6 @@
     for m in step1:
         m.start()
     near.start()
-    for m in moves[1] + moves[2]:
-        m.start()
 
     def keep(w, cb, half):
         for k in range(HALF):
@@ -396,7 +400,8 @@
             for i in range(4):
                 fx[first + half, 4, i] = f[i][8 * half : 8 * half + 8, :]
 
-    load_own.wait()
+    for m in (load_fw, load_tw, load_own, load_iv, load_it):
+        m.wait()
 
     def own(p, _):
         whole_block(rec, p)
@@ -413,7 +418,7 @@
     step2 = [pltpu.make_async_remote_copy(
         src_ref=recv2.at[line], dst_ref=recv2.at[line], send_sem=send2.at[i], recv_sem=got2.at[i],
         device_id=d, device_id_type=MESH) for i, d in enumerate(l_id)]
-    for m in step2:
+    for m in step2 + moves[1] + moves[2]:
         m.start()
 
     near.wait()
@@ -456,6 +461,22 @@
 
     lax.fori_loop(0, 2, source_block, 0)
 
+    for c in range(2):
+        for m in moves[c]:
+            m.wait()
+
+        def two(i, _):
+            whole_block(2 * (1 - pair) + i, c)
+            return 0
+
+        lax.fori_loop(0, 2, two, 0)
+
+    for m in moves[2]:
+        m.wait()
+    half_block(2 * (1 - pair))
+
+
+def correlate_kernel(xs, fx, ss, fs, iv_ref, tw_ref, out_ref, y, z, obuf, osem):
     def send(slot, cb, sp):
         return [pltpu.make_async_copy(
             obuf.at[slot, half],
@@ -485,21 +506,7 @@
             c.start()
         return 0
 
-    for c in range(2):
-        for m in moves[c]:
-            m.wait()
-
-        def two(i, _):
-            whole_block(2 * (1 - pair) + i, c)
-            return 0
-
-        lax.fori_loop(0, 2, two, 0)
-        lax.fori_loop(8 * c, 8 * c + 8, unit, 0)
-
-    for m in moves[2]:
-        m.wait()
-    half_block(2 * (1 - pair))
-    lax.fori_loop(16, 20, unit, 0)
+    lax.fori_loop(0, 20, unit, 0)
     for u in (18, 19):
         for c in send(u % 2, u // 4, u % 4):
             c.wait()
@@ -509,15 +516,26 @@
     fw, iv, tw = tables()
     channels = samples.shape[2]
     vmem = pl.BlockSpec(memory_space=pltpu.VMEM)
-    anywhere = pl.BlockSpec(memory_space=pl.ANY)
+    hbm = pl.BlockSpec(memory_space=pltpu.HBM)
     f32, bf16 = jnp.float32, jnp.bfloat16
     dma = pltpu.SemaphoreType.DMA
-    return pl.pallas_call(
-        kernel,
-        out_shape=jax.ShapeDtypeStruct((NSRC, channels, NFFT), f32),
-        in_specs=[pl.BlockSpec(memory_space=pltpu.SMEM), anywhere, anywhere, vmem, vmem, vmem],
-        out_specs=anywhere,
+    twist, square = pltpu.VMEM((HALF, 2, 8, FAST), f32), pltpu.VMEM((512, 256), bf16)
+    spectra = pl.pallas_call(
+        gather_kernel,
+        out_shape=[
+            jax.ShapeDtypeStruct((NWIN, 5, HALF, 8, 256), f32),
+            jax.ShapeDtypeStruct((NWIN, 5, 4, 8, FAST), f32),
+            jax.ShapeDtypeStruct((NWIN, 4, HALF, 16, 256), f32),
+            jax.ShapeDtypeStruct((NWIN, 4, 4, 16, FAST), f32),
+            jax.ShapeDtypeStruct((512, 256), bf16),
+            jax.ShapeDtypeStruct((HALF, 2, 8, FAST), f32),
+        ],
+        in_specs=[hbm] * 7,
+        out_specs=[vmem] * 6,
         scratch_shapes=[
+            pltpu.SMEM((NSRC,), jnp.int32),
+            square,
+            twist,
             pltpu.VMEM((ROWS, 256), f32),
             pltpu.VMEM((ROWS, 256), f32),
             pltpu.VMEM((4 * channels, NFFT), bf16),
@@ -526,17 +544,25 @@
             pltpu.VMEM((GROUP, NSRC, PIECE), f32),
             pltpu.VMEM((LINE, NSRC, PIECE), f32),
             pltpu.VMEM((GROUP, NWIN * NSRC, PIECE), bf16),
-            pltpu.VMEM((NWIN, 5, HALF, 8, 256), f32),
-            pltpu.VMEM((NWIN, 5, 4, 8, FAST), f32),
-            pltpu.VMEM((NWIN, 4, HALF, 16, 256), f32),
-            pltpu.VMEM((NWIN, 4, 4, 16, FAST), f32),
+            dma((5,)), dma, dma, dma((7,)), dma((7,)), dma((15,)), dma((15,)), dma((7,)), dma((7,)), dma((15,)), dma((15,)),
+        ],
+        compiler_params=pltpu.CompilerParams(
+            collective_id=0, has_side_effects=True, vmem_limit_bytes=32 * 2**20),
+    )(*[pltpu.with_memory_space_constraint(jnp.asarray(a), pltpu.HBM) for a in (
+        source_ids, samples[0], samples.reshape(4 * channels, NFFT), fw, tw[:, 0:2], iv, tw[:, 2:4])])
+    return pl.pallas_call(
+        correlate_kernel,
+        out_shape=jax.ShapeDtypeStruct((NSRC, channels, NFFT), f32),
+        in_specs=[vmem] * 6,
+        out_specs=hbm,
+        scratch_shapes=[
+            pltpu.VMEM((ROWS, 256), f32),
+            pltpu.VMEM((ROWS, 256), f32),
             pltpu.VMEM((2, 2, 8, NFFT), f32),
-            dma, dma, dma((7,)), dma((7,)), dma((15,)), dma((15,)), dma((7,)), dma((7,)), dma((15,)), dma((15,)),
             dma((2, 2)),
         ],
-        compiler_params=pltpu.CompilerParams(
-            collective_id=0, has_side_effects=True, vmem_limit_bytes=48 * 2**20),
-    )(source_ids, samples[0], samples.reshape(4 * channels, NFFT), fw, iv, tw)
+        compiler_params=pltpu.CompilerParams(vmem_limit_bytes=32 * 2**20),
+    )(*spectra)
 
 
 def solution(mesh):

time: 71.9 us -> 47.2 us (0.66)
  local copies, waits for them, and re-layouts: 12.5 us -> 0 us
  Pallas kernels: 59.1 us -> 47.1 us
    unnamed x11 -> x0, local copies, waits for them, and re-layouts: 12.5 us -> none
    pallas_call x1 -> x2, Pallas kernels: 59.1 us -> 47.1 us  [the longest x1 33.2 us: shards(): pl.pallas_call(gather_kernel, out_shape=[jax.ShapeDtypeStruct((NWIN, 5, H...]
where the time goes in v3:
time: 47.2 us; the launch traced here: 47.1 us
  Pallas kernels  47.1 us (100%)
    pallas_call x1, Pallas kernels, shards(): pl.pallas_call(gather_kernel, out_shape=[jax.ShapeDtypeStruct((NWIN, 5, H...  33.2 us
    pallas_call x1, Pallas kernels, shards(): pl.pallas_call(correlate_kernel, out_shape=jax.ShapeDtypeStruct((NSRC, ch...  13.9 us

profile of v3, /device:TPU:1, one launch (start us, length us, event | category | flops | bytes accessed | tf_op | source)
XLA Modules:
  0.0 47.1 jit_solution(12492639944843517842)
XLA Ops:
  0.0 33.2 %shard_map.64 = (f32[4,5,25,8,256]{4,3,2,1,0:T(8,128)S(1)}, f32[4,5,4,8,128]{4,3,2,1,0:T(8,128)S(1)}, f32[4,4,25,16,256]{4,3,2,1,0:T(8,128)S(1)}, f32[4,4,4,16,1...) custom-call(s32[8]{0:T(128)} %ids_hbm.1, bf16[4,40,6144]{2,1,0:T(8,128)(2,1)} %bitcast.2, ...), custom_call_target="tpu_custom_call" | custom-call | tf_op jit(solution)/shard_map/pallas_call | solution.py:523
  33.2 13.9 %shard_map.65 = f32[8,40,6144]{2,1,0:T(8,128)} custom-call(f32[4,5,25,8,256]{4,3,2,1,0:T(8,128)S(1)} %get-tuple-element.11.xs, f32[4,5,4,8,128]{4,3,2,1,0:T(8,128)S(1)} %get-tuple-element.12.fx, f32[4,4,25,16,256]{4,3,2,1,0:T(8,128)S(1)} %get-tuple-element.13.ss, f32[4,4,4,16,128]{4,3,2,1,0:T(8,128)S(1)} %get-tuple-element.14.fs, ...), custom_call_target="tpu_custom_call" | custom-call | tf_op jit(solution)/shard_map/pallas_call | solution.py:553

commit v4 on v3

--- a/solution.py
+++ b/solution.py
@@ -307,6 +307,8 @@
         bins.append((V(real), None if k in (0, 24) else V(re * s + im * c)))
     for j, x in enumerate(slow_inverse(bins)):
         store(j, x.get())
+EARLY = 8
+SLOTS = 3
 GROUP = 16
 LINE = 8
 PIECE = NFFT // GROUP
@@ -314,7 +316,7 @@
 MESH = pl.DeviceIdType.MESH
 
 
-def gather_kernel(ids_hbm, x_ref, flat_ref, fw_hbm, tw_hbm, iv_hbm, it_hbm, xs, fx, ss, fs, iv_ref, it_ref,
+def gather_kernel(ids_hbm, x_ref, flat_ref, fw_hbm, tw_hbm, iv_hbm, it_hbm, xs, fx, ss, fs, iv_ref, it_ref, early,
                   ids_ref, fw_ref, tw_ref, y, z, flat, recvx, part, recv1, recv2, srcs,
                   load_sem, flat_sem, own_sem, send_x, recv_x, send1, got1, send2, got2, send3, got3):
     rec, ch = lax.axis_index("rec"), lax.axis_index("ch")
@@ -329,13 +331,15 @@
     l_id = [(p % 4, q * 2 + p // 4) for p in l_peer]
 
     load_ids = pltpu.make_async_copy(ids_hbm, ids_ref, load_sem.at[0])
-    load_flat = pltpu.make_async_copy(flat_ref, flat, flat_sem)
+    quarter = NFFT // 4
+    load_flat = [pltpu.make_async_copy(flat_ref.at[:, pl.ds(quarter * j, quarter)], flat.at[j], flat_sem.at[j]) for j in range(4)]
     load_fw = pltpu.make_async_copy(fw_hbm, fw_ref, load_sem.at[1])
     load_tw = pltpu.make_async_copy(tw_hbm, tw_ref, load_sem.at[2])
     load_own = pltpu.make_async_copy(x_ref.at[rec], recvx.at[rec], own_sem)
     load_iv = pltpu.make_async_copy(iv_hbm, iv_ref, load_sem.at[3])
     load_it = pltpu.make_async_copy(it_hbm, it_ref, load_sem.at[4])
-    for m in (load_ids, load_flat, load_fw, load_tw, load_own, load_iv, load_it):
+    load_ids.start()
+    for m in load_flat:
         m.start()
     barrier = pltpu.get_barrier_semaphore()
     for d in q_id + l_id:
@@ -359,21 +363,23 @@
         ids = jnp.where(row == s, ids_ref[s], ids)
     here = (col // 40) * 1280 + ch * 40 + col % 40
     chooser = jnp.where(ids == here, 1.0, 0.0).astype(jnp.bfloat16)
-    load_flat.wait()
     for j in range(GROUP):
-        part[j] = jnp.dot(chooser, flat[:, pl.ds(PIECE * j, PIECE)], preferred_element_type=jnp.float32)
+        if j % 4 == 0:
+            load_flat[j // 4].wait()
+        part[j] = jnp.dot(chooser, flat[j // 4, :, pl.ds(PIECE * (j % 4), PIECE)], preferred_element_type=jnp.float32)
     recv1[q] = part[q]
 
     pl.semaphore_wait(barrier, GROUP - 1 + LINE - 1)
 
-    for m in moves[0]:
-        m.start()
+    moves[0][0].start()
     step1 = [pltpu.make_async_remote_copy(
         src_ref=part.at[p], dst_ref=recv1.at[q], send_sem=send1.at[i], recv_sem=got1.at[i],
         device_id=d, device_id_type=MESH) for i, (p, d) in enumerate(zip(q_peer, q_id))]
     for m in step1:
         m.start()
     near.start()
+    for m in (load_fw, load_tw, load_own, load_iv, load_it):
+        m.start()
 
     def keep(w, cb, half):
         for k in range(HALF):
@@ -418,7 +424,7 @@
     step2 = [pltpu.make_async_remote_copy(
         src_ref=recv2.at[line], dst_ref=recv2.at[line], send_sem=send2.at[i], recv_sem=got2.at[i],
         device_id=d, device_id_type=MESH) for i, d in enumerate(l_id)]
-    for m in step2 + moves[1] + moves[2]:
+    for m in step2 + moves[0][1:] + moves[1] + moves[2]:
         m.start()
 
     near.wait()
@@ -438,6 +444,18 @@
     for m in step3:
         m.start()
     half_block(2 * pair)
+
+    def far_chunk(n):
+        for m in moves[n]:
+            m.wait()
+
+        def two(i, _):
+            whole_block(2 * (1 - pair) + i, n)
+            return 0
+
+        lax.fori_loop(0, 2, two, 0)
+
+    far_chunk(0)
     for m in step3:
         m.wait()
 
@@ -461,22 +479,38 @@
 
     lax.fori_loop(0, 2, source_block, 0)
 
-    for c in range(2):
-        for m in moves[c]:
-            m.wait()
-
-        def two(i, _):
-            whole_block(2 * (1 - pair) + i, c)
-            return 0
-
-        lax.fori_loop(0, 2, two, 0)
-
+    def unit(u, _):
+        cb, sp = u // 4, u % 4
+
+        def store(j, x):
+            for half in range(2):
+                early[2 * sp + half, pl.ds(pl.multiple_of(8 * cb, 8), 8), pl.ds(FAST * j, FAST)] = x[8 * half : 8 * half + 8]
+
+        correlate_unit(cb, sp, xs, fx, ss, fs, it_ref, iv_ref, y, z, store)
+        return 0
+
+    lax.fori_loop(0, EARLY, unit, 0)
+    far_chunk(1)
     for m in moves[2]:
         m.wait()
     half_block(2 * (1 - pair))
 
 
-def correlate_kernel(xs, fx, ss, fs, iv_ref, tw_ref, out_ref, y, z, obuf, osem):
+def correlate_unit(cb, sp, xs, fx, ss, fs, tw_ref, iv_ref, y, z, store):
+    cross_inverse(
+        lambda w, k: (xs[w, cb, k, :, 0:128], xs[w, cb, k, :, 128:256]),
+        lambda w: [fx[w, cb, i] for i in range(4)],
+        lambda w, k: (ss[w, sp, k, :, 0:128], ss[w, sp, k, :, 128:256]),
+        lambda w: [fs[w, sp, i] for i in range(4)],
+        tw_ref, iv_ref, y, z, store)
+
+
+def correlate_kernel(xs, fx, ss, fs, iv_ref, tw_ref, early, out_ref, y, z, obuf, osem, early_sem):
+    rows = 2 * EARLY
+    copies = [pltpu.make_async_copy(early.at[s], out_ref.at[s, pl.ds(0, rows), :], early_sem.at[s]) for s in range(NSRC)]
+    for m in copies:
+        m.start()
+
     def send(slot, cb, sp):
         return [pltpu.make_async_copy(
             obuf.at[slot, half],
@@ -485,31 +519,49 @@
 
     def unit(u, _):
         cb, sp = u // 4, u % 4
-        slot = u % 2
-
-        @pl.when(u >= 2)
+        slot = u % SLOTS
+
+        @pl.when(u >= EARLY + SLOTS)
         def _():
-            for c in send(slot, (u - 2) // 4, (u - 2) % 4):
-                c.wait()
+            for m in send(slot, (u - SLOTS) // 4, (u - SLOTS) % 4):
+                m.wait()
 
         def store(j, x):
-            obuf[slot, 0, :, pl.ds(FAST * j, FAST)] = x[0:8]
-            obuf[slot, 1, :, pl.ds(FAST * j, FAST)] = x[8:16]
-
-        cross_inverse(
-            lambda w, k: (xs[w, cb, k, :, 0:128], xs[w, cb, k, :, 128:256]),
-            lambda w: [fx[w, cb, i] for i in range(4)],
-            lambda w, k: (ss[w, sp, k, :, 0:128], ss[w, sp, k, :, 128:256]),
-            lambda w: [fs[w, sp, i] for i in range(4)],
-            tw_ref, iv_ref, y, z, store)
-        for c in send(slot, cb, sp):
-            c.start()
+            for half in range(2):
+                obuf[slot, half, :, pl.ds(FAST * j, FAST)] = x[8 * half : 8 * half + 8]
+
+        correlate_unit(cb, sp, xs, fx, ss, fs, tw_ref, iv_ref, y, z, store)
+        for m in send(slot, cb, sp):
+            m.start()
         return 0
 
-    lax.fori_loop(0, 20, unit, 0)
-    for u in (18, 19):
-        for c in send(u % 2, u // 4, u % 4):
-            c.wait()
+    lax.fori_loop(EARLY, 20, unit, 0)
+    for u in range(20 - SLOTS, 20):
+        for m in send(u % SLOTS, u // 4, u % 4):
+            m.wait()
+    for m in copies:
+        m.wait()
+
+
+def correlate(spectra, iv, tw, early):
+    channels = 8 * spectra[0].shape[1]
+    vmem = pl.BlockSpec(memory_space=pltpu.VMEM)
+    hbm = pl.BlockSpec(memory_space=pltpu.HBM)
+    f32, dma = jnp.float32, pltpu.SemaphoreType.DMA
+    return pl.pallas_call(
+        correlate_kernel,
+        out_shape=jax.ShapeDtypeStruct((NSRC, channels, NFFT), f32),
+        in_specs=[vmem] * 7,
+        out_specs=hbm,
+        scratch_shapes=[
+            pltpu.VMEM((ROWS, 256), f32),
+            pltpu.VMEM((ROWS, 256), f32),
+            pltpu.VMEM((SLOTS, 2, 8, NFFT), f32),
+            dma((SLOTS, 2)),
+            dma((NSRC,)),
+        ],
+        compiler_params=pltpu.CompilerParams(vmem_limit_bytes=32 * 2**20),
+    )(*spectra, iv, tw, early)
 
 
 def shards(samples, source_ids):
@@ -529,40 +581,29 @@
             jax.ShapeDtypeStruct((NWIN, 4, 4, 16, FAST), f32),
             jax.ShapeDtypeStruct((512, 256), bf16),
             jax.ShapeDtypeStruct((HALF, 2, 8, FAST), f32),
+            jax.ShapeDtypeStruct((NSRC, 2 * EARLY, NFFT), f32),
         ],
         in_specs=[hbm] * 7,
-        out_specs=[vmem] * 6,
+        out_specs=[vmem] * 7,
         scratch_shapes=[
             pltpu.SMEM((NSRC,), jnp.int32),
             square,
             twist,
             pltpu.VMEM((ROWS, 256), f32),
             pltpu.VMEM((ROWS, 256), f32),
-            pltpu.VMEM((4 * channels, NFFT), bf16),
+            pltpu.VMEM((4, 4 * channels, NFFT // 4), bf16),
             pltpu.VMEM((NWIN, channels, NFFT), bf16),
             pltpu.VMEM((GROUP, NSRC, PIECE), f32),
             pltpu.VMEM((GROUP, NSRC, PIECE), f32),
             pltpu.VMEM((LINE, NSRC, PIECE), f32),
             pltpu.VMEM((GROUP, NWIN * NSRC, PIECE), bf16),
-            dma((5,)), dma, dma, dma((7,)), dma((7,)), dma((15,)), dma((15,)), dma((7,)), dma((7,)), dma((15,)), dma((15,)),
+            dma((5,)), dma((4,)), dma, dma((7,)), dma((7,)), dma((15,)), dma((15,)), dma((7,)), dma((7,)), dma((15,)), dma((15,)),
         ],
         compiler_params=pltpu.CompilerParams(
             collective_id=0, has_side_effects=True, vmem_limit_bytes=32 * 2**20),
     )(*[pltpu.with_memory_space_constraint(jnp.asarray(a), pltpu.HBM) for a in (
         source_ids, samples[0], samples.reshape(4 * channels, NFFT), fw, tw[:, 0:2], iv, tw[:, 2:4])])
-    return pl.pallas_call(
-        correlate_kernel,
-        out_shape=jax.ShapeDtypeStruct((NSRC, channels, NFFT), f32),
-        in_specs=[vmem] * 6,
-        out_specs=hbm,
-        scratch_shapes=[
-            pltpu.VMEM((ROWS, 256), f32),
-            pltpu.VMEM((ROWS, 256), f32),
-            pltpu.VMEM((2, 2, 8, NFFT), f32),
-            dma((2, 2)),
-        ],
-        compiler_params=pltpu.CompilerParams(vmem_limit_bytes=32 * 2**20),
-    )(*spectra)
+    return correlate(spectra[0:4], *spectra[4:7])
 
 
 def solution(mesh):

time: 47.2 us -> 41.9 us (0.89)
  Pallas kernels: 47.1 us -> 41.6 us
    pallas_call x1, Pallas kernels: 13.9 us -> 8.01 us  [correlate(): pl.pallas_call(correlate_kernel, out_shape=jax.ShapeDtypeStruct((NSRC, ch...]
where the time goes in v4:
time: 41.9 us; the launch traced here: 41.6 us
  Pallas kernels  41.6 us (99%)
    pallas_call x1, Pallas kernels, shards(): pl.pallas_call(gather_kernel, out_shape=[jax.ShapeDtypeStruct((NWIN, 5, H...  33.6 us
    pallas_call x1, Pallas kernels, correlate(): pl.pallas_call(correlate_kernel, out_shape=jax.ShapeDtypeStruct((NSRC, ch...  8.01 us

profile of v4, /device:TPU:1, one launch (start us, length us, event | category | flops | bytes accessed | tf_op | source)
XLA Modules:
  0.0 41.6 jit_solution(7147008426797167583)
XLA Ops:
  0.0 33.6 %shard_map.64 = (f32[4,5,25,8,256]{4,3,2,1,0:T(8,128)S(1)}, f32[4,5,4,8,128]{4,3,2,1,0:T(8,128)S(1)}, f32[4,4,25,16,256]{4,3,2,1,0:T(8,128)S(1)}, f32[4,4,4,16,1...) custom-call(s32[8]{0:T(128)} %ids_hbm.1, ...), custom_call_target="tpu_custom_call" | custom-call | tf_op jit(solution)/shard_map/pallas_call | solution.py:575
  33.6 8.0 %shard_map.65 = f32[8,40,6144]{2,1,0:T(8,128)} custom-call(f32[4,5,25,8,256]{4,3,2,1,0:T(8,128)S(1)} %get-tuple-element.12.xs, f32[4,5,4,8,128]{4,3,2,1,0:T(8,128)S(1)} %get-tuple-element.13.fx, f32[4,4,25,16,256]{4,3,2,1,0:T(8,128)S(1)} %get-tuple-element.14.ss, f32[4,4,4,16,128]{4,3,2,1,0:T(8,128)S(1)} %get-tuple-element.15.fs, ...), custom_call_target="tpu_custom_call" | custom-call | tf_op jit(solution)/shard_map/pallas_call | solution.py:551

commit v5 on v4

--- a/solution.py
+++ b/solution.py
@@ -35,7 +35,7 @@
     iv = np.concatenate([ihi, ilo], axis=0)
     k1 = np.arange(HALF)[:, None]
     turn = 2.0 * np.pi * (k1 * n[None, :]) / NFFT
-    scale = ((-1.0) ** k1) / math.sqrt(NWIN * NFFT) * np.where((k1 == 0) | (k1 == SLOW // 2), 1.0, 0.5)
+    scale = ((-1.0) ** k1) / math.sqrt(NWIN * NFFT)
     tw = np.stack([np.cos(turn), np.sin(turn), np.cos(turn) * scale, np.sin(turn) * scale], axis=1)
     tw = np.broadcast_to(tw[:, :, None, :], (HALF, 4, 8, FAST)).astype(np.float32)
     return fw, iv, np.ascontiguousarray(tw)
@@ -116,8 +116,8 @@
         even[k] = (a[0] + b[0], a[1] - b[1])
         odd[k] = turned((a[0] - b[0], a[1] + b[1]), n - k, n)
     k = n // 4
-    even[k] = (zs[k][0].scale(2.0), None)
-    odd[k] = (zs[k][1].scale(-2.0), None)
+    even[k] = (zs[k][0], None)
+    odd[k] = (-zs[k][1], None)
     xe, xo = irfft(even), irfft(odd)
     out = []
     for a, b in zip(xe, xo):
@@ -169,9 +169,9 @@
     for c in range(9):
         x, y, z = get(c, 0), get(c, 1), get(c, 2)
         if c in (0, 8):
-            tr, si = y[0], y[1].scale(2.0 * R3)
-            m = x[0] - tr
-            mid[0][c] = (x[0] + tr.scale(2.0), None)
+            tr, si = y[0], y[1].scale(R3)
+            m = x[0] - tr.scale(0.5)
+            mid[0][c] = (x[0] + tr, None)
             mid[1][c] = (m - si, None)
             mid[2][c] = (m + si, None)
             continue
@@ -322,12 +322,14 @@
     rec, ch = lax.axis_index("rec"), lax.axis_index("ch")
     q, x_hi = ch // 2, ch % 2
     line = x_hi * 4 + rec
-    pair = rec // 2
+    pair, core = rec // 2, rec % 2
     sibling = rec + 1 - 2 * (rec % 2)
     far = [(rec + 2) % 4, (sibling + 2) % 4]
-    q_peer = [(q + i) % GROUP for i in range(1, GROUP)]
+    hops = lambda offset: sum(min(d, 4 - d) for d in offset)
+    offsets = sorted(((a, b) for a in range(4) for b in range(4) if a or b), key=hops, reverse=True)
+    q_peer = [(q // 4 + a) % 4 * 4 + (q % 4 + b) % 4 for a, b in offsets]
     q_id = [(rec, p * 2 + x_hi) for p in q_peer]
-    l_peer = [(line + i) % LINE for i in range(1, LINE)]
+    l_peer = [(line // 2 + i) % 4 * 2 + (line + j) % 2 for i, j in ((2, 0), (2, 1), (1, 0), (3, 0), (1, 1), (3, 1), (0, 1))]
     l_id = [(p % 4, q * 2 + p // 4) for p in l_peer]
 
     load_ids = pltpu.make_async_copy(ids_hbm, ids_ref, load_sem.at[0])
@@ -370,7 +372,6 @@
     recv1[q] = part[q]
 
     pl.semaphore_wait(barrier, GROUP - 1 + LINE - 1)
-
     moves[0][0].start()
     step1 = [pltpu.make_async_remote_copy(
         src_ref=part.at[p], dst_ref=recv1.at[q], send_sem=send1.at[i], recv_sem=got1.at[i],
@@ -416,7 +417,7 @@
     lax.fori_loop(0, 2, own, 0)
 
     for m in step1:
-        m.wait()
+        m.wait_recv()
     total = recv1[0]
     for j in range(1, GROUP):
         total = total + recv1[j]
@@ -427,7 +428,7 @@
     for m in step2 + moves[0][1:] + moves[1] + moves[2]:
         m.start()
 
-    near.wait()
+    near.wait_recv()
 
     def second(p, _):
         whole_block(sibling, p)
@@ -436,10 +437,11 @@
     lax.fori_loop(0, 2, second, 0)
 
     for m in step2:
-        m.wait()
-    srcs[q] = jnp.concatenate([recv2[w] + recv2[4 + w] for w in range(NWIN)], axis=0).astype(jnp.bfloat16)
+        m.wait_recv()
+    srcs[core, q] = jnp.concatenate(
+        [recv2[2 * core + i] + recv2[4 + 2 * core + i] for i in range(2)], axis=0).astype(jnp.bfloat16)
     step3 = [pltpu.make_async_remote_copy(
-        src_ref=srcs.at[q], dst_ref=srcs.at[q], send_sem=send3.at[i], recv_sem=got3.at[i],
+        src_ref=srcs.at[core, q], dst_ref=srcs.at[core, q], send_sem=send3.at[i], recv_sem=got3.at[i],
         device_id=d, device_id_type=MESH) for i, d in enumerate(q_id)]
     for m in step3:
         m.start()
@@ -447,7 +449,7 @@
 
     def far_chunk(n):
         for m in moves[n]:
-            m.wait()
+            m.wait_recv()
 
         def two(i, _):
             whole_block(2 * (1 - pair) + i, n)
@@ -457,13 +459,22 @@
 
     far_chunk(0)
     for m in step3:
-        m.wait()
-
-    def source_block(p, _):
-        rows = pl.ds(pl.multiple_of(16 * p, 16), 16)
+        m.wait_recv()
+
+    share = pltpu.make_async_remote_copy(
+        src_ref=srcs.at[core], dst_ref=srcs.at[core], send_sem=send_x.at[7], recv_sem=recv_x.at[7],
+        device_id=(sibling, ch), device_id_type=MESH)
+    share.start()
+
+    def source_block(i, _):
+        p = (core + i) % 2
+
+        @pl.when(i == 1)
+        def _():
+            share.wait_recv()
 
         def load(n):
-            return srcs[n // 3, rows, pl.ds(FAST * (n % 3), FAST)].astype(jnp.float32)
+            return srcs[p, n // 3, :, pl.ds(FAST * (n % 3), FAST)].astype(jnp.float32)
 
         forward16(load, tw_ref, fw_ref, y, z)
         f = factors(z)
@@ -492,8 +503,10 @@
     lax.fori_loop(0, EARLY, unit, 0)
     far_chunk(1)
     for m in moves[2]:
-        m.wait()
+        m.wait_recv()
     half_block(2 * (1 - pair))
+    for m in step1 + step2 + step3 + moves[0] + moves[1] + moves[2] + [near, share]:
+        m.wait_send()
 
 
 def correlate_unit(cb, sp, xs, fx, ss, fs, tw_ref, iv_ref, y, z, store):
@@ -596,8 +609,8 @@
             pltpu.VMEM((GROUP, NSRC, PIECE), f32),
             pltpu.VMEM((GROUP, NSRC, PIECE), f32),
             pltpu.VMEM((LINE, NSRC, PIECE), f32),
-            pltpu.VMEM((GROUP, NWIN * NSRC, PIECE), bf16),
-            dma((5,)), dma((4,)), dma, dma((7,)), dma((7,)), dma((15,)), dma((15,)), dma((7,)), dma((7,)), dma((15,)), dma((15,)),
+            pltpu.VMEM((2, GROUP, 2 * NSRC, PIECE), bf16),
+            dma((5,)), dma((4,)), dma, dma((8,)), dma((8,)), dma((15,)), dma((15,)), dma((7,)), dma((7,)), dma((15,)), dma((15,)),
         ],
         compiler_params=pltpu.CompilerParams(
             collective_id=0, has_side_effects=True, vmem_limit_bytes=32 * 2**20),

time: 41.9 us -> 41.4 us (0.988)
  no operation moved by 1% of the time
where the time goes in v5:
time: 41.4 us; the launch traced here: 41.2 us
  Pallas kernels  41.2 us (100%)
    pallas_call x1, Pallas kernels, shards(): pl.pallas_call(gather_kernel, out_shape=[jax.ShapeDtypeStruct((NWIN, 5, H...  33.3 us
    pallas_call x1, Pallas kernels, correlate(): pl.pallas_call(correlate_kernel, out_shape=jax.ShapeDtypeStruct((NSRC, ch...  7.9 us

profile of v5, /device:TPU:1, one launch (start us, length us, event | category | flops | bytes accessed | tf_op | source)
XLA Modules:
  0.0 41.2 jit_solution(16477404274657603659)
XLA Ops:
  0.0 33.3 %shard_map.64 = (f32[4,5,25,8,256]{4,3,2,1,0:T(8,128)S(1)}, f32[4,5,4,8,128]{4,3,2,1,0:T(8,128)S(1)}, f32[4,4,25,16,256]{4,3,2,1,0:T(8,128)S(1)}, f32[4,4,4,16,1...) custom-call(s32[8]{0:T(128)} %ids_hbm.1, ...), custom_call_target="tpu_custom_call" | custom-call | tf_op jit(solution)/shard_map/pallas_call | solution.py:588
  33.3 7.9 %shard_map.65 = f32[8,40,6144]{2,1,0:T(8,128)} custom-call(f32[4,5,25,8,256]{4,3,2,1,0:T(8,128)S(1)} %get-tuple-element.12.xs, f32[4,5,4,8,128]{4,3,2,1,0:T(8,128)S(1)} %get-tuple-element.13.fx, f32[4,4,25,16,256]{4,3,2,1,0:T(8,128)S(1)} %get-tuple-element.14.ss, f32[4,4,4,16,128]{4,3,2,1,0:T(8,128)S(1)} %get-tuple-element.15.fs, ...), custom_call_target="tpu_custom_call" | custom-call | tf_op jit(solution)/shard_map/pallas_call | solution.py:564

commit v6 on v5

--- a/solution.py
+++ b/solution.py
@@ -382,16 +382,11 @@
     for m in (load_fw, load_tw, load_own, load_iv, load_it):
         m.start()
 
-    def keep(w, cb, half):
-        for k in range(HALF):
-            xs[w, cb, k] = z[pl.ds(16 * k + 8 * half, 8), :]
-
     def whole_block(w, p):
         rows = pl.ds(pl.multiple_of(16 * p, 16), 16)
-        forward16(lambda n: recvx[w, rows, pl.ds(FAST * n, FAST)].astype(jnp.float32), tw_ref, fw_ref, y, z)
-        f = factors(z)
+        forward16(lambda n: recvx[w, rows, pl.ds(FAST * n, FAST)].astype(jnp.float32), tw_ref, fw_ref, y, xs.at[2 * w + p])
+        f = factors(xs.at[2 * w + p])
         for half in range(2):
-            keep(w, 2 * p + half, half)
             for i in range(4):
                 fx[w, 2 * p + half, i] = f[i][8 * half : 8 * half + 8, :]
 
@@ -400,10 +395,10 @@
             return jnp.concatenate(
                 [recvx[first + half, pl.ds(32, 8), pl.ds(FAST * n, FAST)].astype(jnp.float32) for half in range(2)], axis=0)
 
-        forward16(load, tw_ref, fw_ref, y, z)
-        f = factors(z)
+        block = 8 + first // 2
+        forward16(load, tw_ref, fw_ref, y, xs.at[block])
+        f = factors(xs.at[block])
         for half in range(2):
-            keep(first + half, 4, half)
             for i in range(4):
                 fx[first + half, 4, i] = f[i][8 * half : 8 * half + 8, :]
 
@@ -510,8 +505,13 @@
 
 
 def correlate_unit(cb, sp, xs, fx, ss, fs, tw_ref, iv_ref, y, z, store):
+    def load_x(w, k):
+        block = jnp.where(cb < 4, 2 * w + cb // 2, 8 + w // 2)
+        rows = pl.ds(pl.multiple_of(16 * k + 8 * jnp.where(cb < 4, cb % 2, w % 2), 8), 8)
+        return xs[block, rows, 0:128], xs[block, rows, 128:256]
+
     cross_inverse(
-        lambda w, k: (xs[w, cb, k, :, 0:128], xs[w, cb, k, :, 128:256]),
+        load_x,
         lambda w: [fx[w, cb, i] for i in range(4)],
         lambda w, k: (ss[w, sp, k, :, 0:128], ss[w, sp, k, :, 128:256]),
         lambda w: [fs[w, sp, i] for i in range(4)],
@@ -557,7 +557,7 @@
 
 
 def correlate(spectra, iv, tw, early):
-    channels = 8 * spectra[0].shape[1]
+    channels = 8 * spectra[1].shape[1]
     vmem = pl.BlockSpec(memory_space=pltpu.VMEM)
     hbm = pl.BlockSpec(memory_space=pltpu.HBM)
     f32, dma = jnp.float32, pltpu.SemaphoreType.DMA
@@ -588,7 +588,7 @@
     spectra = pl.pallas_call(
         gather_kernel,
         out_shape=[
-            jax.ShapeDtypeStruct((NWIN, 5, HALF, 8, 256), f32),
+            jax.ShapeDtypeStruct((12, ROWS, 256), f32),
             jax.ShapeDtypeStruct((NWIN, 5, 4, 8, FAST), f32),
             jax.ShapeDtypeStruct((NWIN, 4, HALF, 16, 256), f32),
             jax.ShapeDtypeStruct((NWIN, 4, 4, 16, FAST), f32),

time: 41.4 us -> 41.4 us (level)
  no operation moved by 1% of the time
where the time goes in v6:
time: 41.4 us; the launch traced here: 41.3 us
  Pallas kernels  41.3 us (100%)
    pallas_call x1, Pallas kernels, shards(): pl.pallas_call(gather_kernel, out_shape=[jax.ShapeDtypeStruct((12, ROWS,...  33.3 us
    pallas_call x1, Pallas kernels, correlate(): pl.pallas_call(correlate_kernel, out_shape=jax.ShapeDtypeStruct((NSRC, ch...  7.98 us

profile of v6, /device:TPU:1, one launch (start us, length us, event | category | flops | bytes accessed | tf_op | source)
XLA Modules:
  0.0 41.3 jit_solution(7780760031949528299)
XLA Ops:
  0.0 33.3 %shard_map.64 = (f32[12,400,256]{2,1,0:T(8,128)S(1)}, f32[4,5,4,8,128]{4,3,2,1,0:T(8,128)S(1)}, f32[4,4,25,16,256]{4,3,2,1,0:T(8,128)S(1)}, f32[4,4,4,16,128]{4,...) custom-call(s32[8]{0:T(128)} %ids_hbm.1, ...), custom_call_target="tpu_custom_call" | custom-call | tf_op jit(solution)/shard_map/pallas_call | solution.py:588
  33.3 8.0 %shard_map.65 = f32[8,40,6144]{2,1,0:T(8,128)} custom-call(f32[12,400,256]{2,1,0:T(8,128)S(1)} %get-tuple-element.12.xs, f32[4,5,4,8,128]{4,3,2,1,0:T(8,128)S(1)} %get-tuple-element.13.fx, f32[4,4,25,16,256]{4,3,2,1,0:T(8,128)S(1)} %get-tuple-element.14.ss, f32[4,4,4,16,128]{4,3,2,1,0:T(8,128)S(1)} %get-tuple-element.15.fs, ...), custom_call_target="tpu_custom_call" | custom-call | tf_op jit(solution)/shard_map/pallas_call | solution.py:564
